TPU v7x, 256 devices: a whole 4x4x8 slice. The times are simulated.
256 devices in a mesh: grp: 16 (over x_lo, z), blk: 16 (over y, x_hi, core).
Axes of the slice: x: 4 (x_hi: 2, x_lo: 2; x = x_hi * 2 + x_lo), y: 4, z: 8, core: 2. Of those that a mesh axis runs over, the one named last changes fastest.
Arguments:
- image_emb: bfloat16 [32768, 1152], P(('grp', 'blk')), may hold values from -6 to 6
- text_hidden: bfloat16 [32768, 4304], P(('grp', 'blk')), may hold values from -6 to 6
- head_weight: bfloat16 [4304, 1152], replicated, may hold values from -0.09375 to 0.09375
- positive: int32 [256, 128], P(('grp', 'blk')), may hold values from 0 to 127, each once within a row
- log_scale: float32 [1], replicated, may hold values from 4 to 4.5
- bias: float32 [1], replicated, may hold values from -9 to -6
Outputs:
- image_grad: float32 [32768, 1152], P(('grp', 'blk'))
- head_grad: float32 [4304, 1152], P('blk', 'grp')
Inputs may be any that keep to these rules, and one draw needn't show every extreme that they name: Each row of positive is a permutation of the 128 rows of one device: image r of a device is paired with text positive[., r] of the same device.
All inputs are finite; a program needn't handle non-finite values.
Results may differ from a plain program's by a relative error of at most 0.038.
Values may be sent and summed in bfloat16 or wider, within the bound.
A program may use at most 64 MiB of HBM per device.

v0:
```python
import jax
import jax.numpy as jnp
from jax import lax
from jax.sharding import PartitionSpec as P


def shifted(value, axis, steps):
    count = lax.axis_size(axis)
    pairs = [(source, (source + steps) % count) for source in range(count)]
    return lax.ppermute(value, axis, pairs)


def normalize(raw_values):
    norm_value = jnp.sqrt(jnp.sum(raw_values * raw_values, axis=-1, keepdims=True) + 1e-06)
    return (norm_value, raw_values / norm_value)


def unit_back(direction, incoming, norm_value):
    along = jnp.sum(direction * incoming, axis=-1, keepdims=True)
    return (incoming - direction * along) / norm_value


def contract_first(weight, values):
    return lax.dot_general(
        weight, values, (((0,), (0,)), ((), ())), preferred_element_type=jnp.float32
    )


def pair_weights(left_units, right_units, labels, logit_scale, logit_bias):
    logits = (
        logit_scale
        * lax.dot_general(
            left_units, right_units, (((1,), (1,)), ((), ())), preferred_element_type=jnp.float32
        )
        + logit_bias
    )
    return (logit_scale * (jax.nn.sigmoid(logits) - labels)).astype(jnp.bfloat16)


def pass_sums(carried):
    return shifted(carried.astype(jnp.bfloat16), "blk", 1).astype(carried.dtype)


def local(image_emb, text_hidden, head_weight, positive, log_scale, bias):
    blocks = lax.axis_size("blk")
    row_count = image_emb.shape[0]
    logit_scale = jnp.exp(log_scale[0])
    logit_bias = bias[0]
    image_norm, image_dir = normalize(image_emb.astype(jnp.float32))
    image_unit = image_dir.astype(jnp.bfloat16)
    text_raw = jnp.dot(text_hidden, head_weight, preferred_element_type=jnp.float32)
    text_norm, text_dir = normalize(text_raw)
    text_unit = text_dir.astype(jnp.bfloat16)
    columns = jnp.arange(row_count, dtype=jnp.int32)
    labels = (positive[0][:, None] == columns[None, :]).astype(jnp.float32)
    local_weight = pair_weights(image_unit, text_unit, labels, logit_scale, logit_bias)
    image_acc = jnp.dot(local_weight, text_unit, preferred_element_type=jnp.float32)
    text_acc = contract_first(local_weight, image_unit)

    def visit_carried(visit_index, loop_state):
        text_panel, carried, image_sum = loop_state
        text_panel = shifted(text_panel, "blk", 1)
        carried = pass_sums(carried)
        weight = pair_weights(image_unit, text_panel, 0.0, logit_scale, logit_bias)
        image_sum = image_sum + jnp.dot(weight, text_panel, preferred_element_type=jnp.float32)
        carried = carried + contract_first(weight, image_unit)
        return (text_panel, carried, image_sum)

    final_state = lax.fori_loop(0, blocks - 1, visit_carried, (text_unit, text_acc, image_acc))
    image_acc = final_state[2]
    text_acc = pass_sums(final_state[1])
    image_grad = unit_back(image_dir, image_acc, image_norm)
    text_raw_grad = unit_back(text_dir, text_acc, text_norm).astype(jnp.bfloat16)
    head_block = lax.psum_scatter(
        contract_first(text_hidden, text_raw_grad).astype(jnp.bfloat16),
        "blk",
        scatter_dimension=0,
        tiled=True,
    )
    head_grad = lax.psum_scatter(head_block, "grp", scatter_dimension=1, tiled=True).astype(
        jnp.float32
    )
    return (image_grad, head_grad)


def solution(mesh):
    in_specs = (
        P(("grp", "blk"), None),
        P(("grp", "blk"), None),
        P(),
        P(("grp", "blk"), None),
        P(),
        P(),
    )
    out_specs = (P(("grp", "blk"), None), P("blk", "grp"))
    return jax.shard_map(local, mesh=mesh, in_specs=in_specs, out_specs=out_specs, check_vma=False)
```

profile of v0, /device:TPU:1, one launch (start us, length us, event | category | flops | bytes accessed | tf_op | source)
XLA Modules:
  0.0 505.7 jit_solution(18289015648274165602)
XLA Ops:
  7.2 1.2 fusion.17
  8.5 5.6 %multiply_reduce_fusion.1 = (f32[128]{0:T(128)S(1)}, f32[128,1152]{1,0:T(8,128)S(1)}) fusion(bf16[128,4304]{0,1:T(8,128)(2,1)S(1)} %copy-done, bf16[4304,1152]{1,0:T(8,128)(2,1)} %param.10), kind=kOutput, calls=%fused_computation.31 | convolution fusion | flops 1269596032 | bytes 11608576 | tf_op jit(solution)/shard_map/dot_general | solution.py:51
  16.3 1.2 fusion.16
  17.6 1.0 fusion.26
  18.6 1.2 fusion.27
  19.7 209.7 %while.14 = (s32[]{:T(128)}, bf16[128,1152]{1,0:T(8,128)(2,1)}, bf16[128,1152]{1,0:T(8,128)(2,1)}, f32[128,1152]{1,0:T(8,128)S(1)}, f32[]{:T(128)}, /*index=5*/bf16[128,1152]{1,0:T(8,128)(2,1)S(1)}, f32[]{:T(128)}, s32[]{:T(128)}) while((s32[]{:T(128)}, bf16[128,1152]{1,0:T(8,128)(2,1)}, bf16[128,1152]{1,0:T(8,128)(2,1)}, ...), condition=%wide.region_3.0_spmd, body=%wide.region_2.0_spmd.sunk | while | flops 113950720 | bytes 5996717 | solution.py:69
  19.8 4.2 collective-permute-start
  24.1 3.9 collective-permute-done
  28.7 0.9 fusion.56
  29.6 1.5 collective-permute-done.1
  31.1 1.0 convert_add_fusion.2
  32.3 4.0 collective-permute-start
  36.4 3.9 collective-permute-done
  41.0 0.9 fusion.56
  41.9 1.5 collective-permute-done.1
  43.4 1.0 convert_add_fusion.2
  44.7 4.0 collective-permute-start
  48.7 4.5 collective-permute-done
  54.0 0.9 fusion.56
  54.9 0.9 collective-permute-done.1
  55.8 1.0 convert_add_fusion.2
  57.0 4.0 collective-permute-start
  61.1 6.6 %collective-permute-done = bf16[128,1152]{1,0:T(8,128)(2,1)S(1)} collective-permute-done((bf16[128,1152]{1,0:T(8,128)(2,1)}, bf16[128,1152]{1,0:T(8,128)(2,1)S(1)}, u32[]{:S(2)}, u32[]{:S(2)}) %collective-permute-start) | collective-permute-done | bytes 294944 | tf_op jit(solution)/shard_map/while/body/eval_jaxpr/ppermute | solution.py:10
  69.3 1.0 convert_add_fusion.2
  70.6 2.8 collective-permute-start
  73.8 8.4 %collective-permute-done = bf16[128,1152]{1,0:T(8,128)(2,1)S(1)} collective-permute-done((bf16[128,1152]{1,0:T(8,128)(2,1)}, bf16[128,1152]{1,0:T(8,128)(2,1)S(1)}, u32[]{:S(2)}, u32[]{:S(2)}) %collective-permute-start) | collective-permute-done | bytes 294944 | tf_op jit(solution)/shard_map/while/body/eval_jaxpr/ppermute | solution.py:10
  82.8 0.9 fusion.56
  83.8 1.0 convert_add_fusion.2
  85.6 1.3 collective-permute-start.1
  87.0 9.6 %collective-permute-done = bf16[128,1152]{1,0:T(8,128)(2,1)S(1)} collective-permute-done((bf16[128,1152]{1,0:T(8,128)(2,1)}, bf16[128,1152]{1,0:T(8,128)(2,1)S(1)}, u32[]{:S(2)}, u32[]{:S(2)}) %collective-permute-start) | collective-permute-done | bytes 294944 | tf_op jit(solution)/shard_map/while/body/eval_jaxpr/ppermute | solution.py:10
  97.3 0.9 fusion.56
  98.2 1.0 convert_add_fusion.2
  100.2 10.8 %collective-permute-done = bf16[128,1152]{1,0:T(8,128)(2,1)S(1)} collective-permute-done((bf16[128,1152]{1,0:T(8,128)(2,1)}, bf16[128,1152]{1,0:T(8,128)(2,1)S(1)}, u32[]{:S(2)}, u32[]{:S(2)}) %collective-permute-start) | collective-permute-done | bytes 294944 | tf_op jit(solution)/shard_map/while/body/eval_jaxpr/ppermute | solution.py:10
  111.7 0.9 fusion.56
  112.6 1.0 convert_add_fusion.2
  114.1 11.4 %collective-permute-done = bf16[128,1152]{1,0:T(8,128)(2,1)S(1)} collective-permute-done((bf16[128,1152]{1,0:T(8,128)(2,1)}, bf16[128,1152]{1,0:T(8,128)(2,1)S(1)}, u32[]{:S(2)}, u32[]{:S(2)}) %collective-permute-start) | collective-permute-done | bytes 294944 | tf_op jit(solution)/shard_map/while/body/eval_jaxpr/ppermute | solution.py:10
  127.1 1.0 convert_add_fusion.2
  128.5 11.4 %collective-permute-done = bf16[128,1152]{1,0:T(8,128)(2,1)S(1)} collective-permute-done((bf16[128,1152]{1,0:T(8,128)(2,1)}, bf16[128,1152]{1,0:T(8,128)(2,1)S(1)}, u32[]{:S(2)}, u32[]{:S(2)}) %collective-permute-start) | collective-permute-done | bytes 294944 | tf_op jit(solution)/shard_map/while/body/eval_jaxpr/ppermute | solution.py:10
  140.6 0.9 fusion.56
  141.5 1.0 convert_add_fusion.2
  142.9 11.4 %collective-permute-done = bf16[128,1152]{1,0:T(8,128)(2,1)S(1)} collective-permute-done((bf16[128,1152]{1,0:T(8,128)(2,1)}, bf16[128,1152]{1,0:T(8,128)(2,1)S(1)}, u32[]{:S(2)}, u32[]{:S(2)}) %collective-permute-start) | collective-permute-done | bytes 294944 | tf_op jit(solution)/shard_map/while/body/eval_jaxpr/ppermute | solution.py:10
  155.0 0.9 fusion.56
  156.0 1.0 convert_add_fusion.2
  157.4 11.4 %collective-permute-done = bf16[128,1152]{1,0:T(8,128)(2,1)S(1)} collective-permute-done((bf16[128,1152]{1,0:T(8,128)(2,1)}, bf16[128,1152]{1,0:T(8,128)(2,1)S(1)}, u32[]{:S(2)}, u32[]{:S(2)}) %collective-permute-start) | collective-permute-done | bytes 294944 | tf_op jit(solution)/shard_map/while/body/eval_jaxpr/ppermute | solution.py:10
  169.5 0.9 fusion.56
  170.4 1.0 convert_add_fusion.2
  171.8 11.4 %collective-permute-done = bf16[128,1152]{1,0:T(8,128)(2,1)S(1)} collective-permute-done((bf16[128,1152]{1,0:T(8,128)(2,1)}, bf16[128,1152]{1,0:T(8,128)(2,1)S(1)}, u32[]{:S(2)}, u32[]{:S(2)}) %collective-permute-start) | collective-permute-done | bytes 294944 | tf_op jit(solution)/shard_map/while/body/eval_jaxpr/ppermute | solution.py:10
  184.9 1.0 convert_add_fusion.2
  186.3 11.4 %collective-permute-done = bf16[128,1152]{1,0:T(8,128)(2,1)S(1)} collective-permute-done((bf16[128,1152]{1,0:T(8,128)(2,1)}, bf16[128,1152]{1,0:T(8,128)(2,1)S(1)}, u32[]{:S(2)}, u32[]{:S(2)}) %collective-permute-start) | collective-permute-done | bytes 294944 | tf_op jit(solution)/shard_map/while/body/eval_jaxpr/ppermute | solution.py:10
  198.4 0.9 fusion.56
  199.3 1.0 convert_add_fusion.2
  200.7 11.4 %collective-permute-done = bf16[128,1152]{1,0:T(8,128)(2,1)S(1)} collective-permute-done((bf16[128,1152]{1,0:T(8,128)(2,1)}, bf16[128,1152]{1,0:T(8,128)(2,1)S(1)}, u32[]{:S(2)}, u32[]{:S(2)}) %collective-permute-start) | collective-permute-done | bytes 294944 | tf_op jit(solution)/shard_map/while/body/eval_jaxpr/ppermute | solution.py:10
  213.7 1.0 convert_add_fusion.2
  215.2 11.4 %collective-permute-done = bf16[128,1152]{1,0:T(8,128)(2,1)S(1)} collective-permute-done((bf16[128,1152]{1,0:T(8,128)(2,1)}, bf16[128,1152]{1,0:T(8,128)(2,1)S(1)}, u32[]{:S(2)}, u32[]{:S(2)}) %collective-permute-start) | collective-permute-done | bytes 294944 | tf_op jit(solution)/shard_map/while/body/eval_jaxpr/ppermute | solution.py:10
  228.2 1.0 convert_add_fusion.2
  229.5 11.5 %collective-permute-done.2 = bf16[128,1152]{1,0:T(8,128)(2,1)S(1)} collective-permute-done((bf16[128,1152]{1,0:T(8,128)(2,1)}, bf16[128,1152]{1,0:T(8,128)(2,1)S(1)}, u32[]{:S(2)}, u32[]{:S(2)}) %collective-permute-start.2) | collective-permute-done | bytes 294944 | tf_op jit(solution)/shard_map/ppermute | solution.py:10
  241.2 5.7 %fusion.8 = bf16[4304,1152]{1,0:T(8,128)(2,1)} fusion(bf16[128,4304]{0,1:T(8,128)(2,1)S(1)} %copy-done, bf16[128,1152]{1,0:T(8,128)(2,1)S(1)} %collective-permute-done.2, f32[128]{0:T(128)S(1)} %fusion.18, f32[128]{0:T(128)S(1)} %add_sqrt_fusion.1, f32[128,1152]{1,0:T(8,128)S(1)} %get-tuple-element.61), kind=kOutput, calls=%fused_computation.11 | convolution fusion | flops 1275144192 | bytes 11904000 | tf_op jit(solution)/shard_map/dot_general | solution.py:24
  246.9 112.6 %fusion = bf16[272,1152]{1,0:T(8,128)(2,1)S(1)} fusion(bf16[4304,1152]{1,0:T(8,128)(2,1)} %fusion.8), kind=kCustom, calls=%all-reduce-scatter | all-reduce-scatter fusion | flops 5013505 | bytes 10544128
  359.6 5.9 %collective-permute-start.3 = (bf16[45,1152]{1,0:T(8,128)(2,1)S(1)}, bf16[45,1152]{1,0:T(8,128)(2,1)S(1)}, u32[]{:S(2)}, u32[]{:S(2)}) collective-permute-start(bf16[45,1152]{1,0:T(8,128)(2,1)S(1)} %slice), channel_id=1, source_target_pairs={{0,1},{1,2},{2,3},{3,4},{4,5},{5,6},{6,7},{7,8},{8,9},{9,10},{10,1... | collective-permute-start | bytes 311048
  368.0 2.5 concatenate
  370.5 1.0 constant_dynamic-slice_fusion
  371.7 1.0 subtract_divide_fusion
  372.7 124.4 %all-reduce.5.cloned.1.call-done = bf16[269,1152]{1,0:T(8,128)(2,1)} async-done(((bf16[269,1152]{1,0:T(8,128)(2,1)}), bf16[269,1152]{1,0:T(8,128)(2,1)}) %all-reduce.5.cloned.1.call-update) | async-done | bytes 619792
  497.1 1.0 dynamic-slice_convert_fusion
  (94 shorter events, 26.0 us)
Async XLA Ops:
  7.2 1.3 copy-start
  7.2 8.3 %copy-start.1 = (bf16[128,1152]{1,0:T(8,128)(2,1)S(1)}, bf16[128,1152]{1,0:T(8,128)(2,1)}, u32[]{:S(2)}) copy-start(bf16[128,1152]{1,0:T(8,128)(2,1)} %param.8) | copy-start | bytes 884740
  7.2 489.9 %all-reduce.5.cloned.1.call-start = ((), (), s32[]{:S(2)}) async-start(), calls=%async_computation | async-start | bytes 1253376
  8.5 7.8 %copy-start.3 = (s32[1,128]{1,0:T(1,128)S(1)}, s32[1,128]{1,0:T(1,128)}, u32[]{:S(2)}) copy-start(s32[1,128]{1,0:T(1,128)} %param.11) | copy-start | bytes 1540
  19.8 8.2 %collective-permute-start = (bf16[128,1152]{1,0:T(8,128)(2,1)}, bf16[128,1152]{1,0:T(8,128)(2,1)S(1)}, u32[]{:S(2)}, u32[]{:S(2)}) collective-permute-start(bf16[128,1152]{1,0:T(8,128)(2,1)} %get-tuple-element.116), channel_id=1, source_target_pairs={{0,1},{1,2},{2,3},{3,4},{4,5},{5,6},{6,7},{7,8},{8,9},{9,10},{10,1... | collective-permute-start | bytes 884744 | tf_op jit(solution)/shard_map/while/body/eval_jaxpr/ppermute | solution.py:10
  24.0 7.1 %collective-permute-start.1 = (bf16[128,1152]{1,0:T(8,128)(2,1)}, bf16[128,1152]{1,0:T(8,128)(2,1)S(1)}, u32[]{:S(2)}, u32[]{:S(2)}) collective-permute-start(bf16[128,1152]{1,0:T(8,128)(2,1)} %get-tuple-element.117), channel_id=1, source_target_pairs={{0,1},{1,2},{2,3},{3,4},{4,5},{5,6},{6,7},{7,8},{8,9},{9,10},{10,1... | collective-permute-start | bytes 884744 | tf_op jit(solution)/shard_map/while/body/eval_jaxpr/ppermute | solution.py:10
  32.3 7.9 %collective-permute-start = (bf16[128,1152]{1,0:T(8,128)(2,1)}, bf16[128,1152]{1,0:T(8,128)(2,1)S(1)}, u32[]{:S(2)}, u32[]{:S(2)}) collective-permute-start(bf16[128,1152]{1,0:T(8,128)(2,1)} %get-tuple-element.116), channel_id=1, source_target_pairs={{0,1},{1,2},{2,3},{3,4},{4,5},{5,6},{6,7},{7,8},{8,9},{9,10},{10,1... | collective-permute-start | bytes 884744 | tf_op jit(solution)/shard_map/while/body/eval_jaxpr/ppermute | solution.py:10
  36.3 7.1 %collective-permute-start.1 = (bf16[128,1152]{1,0:T(8,128)(2,1)}, bf16[128,1152]{1,0:T(8,128)(2,1)S(1)}, u32[]{:S(2)}, u32[]{:S(2)}) collective-permute-start(bf16[128,1152]{1,0:T(8,128)(2,1)} %get-tuple-element.117), channel_id=1, source_target_pairs={{0,1},{1,2},{2,3},{3,4},{4,5},{5,6},{6,7},{7,8},{8,9},{9,10},{10,1... | collective-permute-start | bytes 884744 | tf_op jit(solution)/shard_map/while/body/eval_jaxpr/ppermute | solution.py:10
  44.7 8.6 %collective-permute-start = (bf16[128,1152]{1,0:T(8,128)(2,1)}, bf16[128,1152]{1,0:T(8,128)(2,1)S(1)}, u32[]{:S(2)}, u32[]{:S(2)}) collective-permute-start(bf16[128,1152]{1,0:T(8,128)(2,1)} %get-tuple-element.116), channel_id=1, source_target_pairs={{0,1},{1,2},{2,3},{3,4},{4,5},{5,6},{6,7},{7,8},{8,9},{9,10},{10,1... | collective-permute-start | bytes 884744 | tf_op jit(solution)/shard_map/while/body/eval_jaxpr/ppermute | solution.py:10
  48.6 7.1 %collective-permute-start.1 = (bf16[128,1152]{1,0:T(8,128)(2,1)}, bf16[128,1152]{1,0:T(8,128)(2,1)S(1)}, u32[]{:S(2)}, u32[]{:S(2)}) collective-permute-start(bf16[128,1152]{1,0:T(8,128)(2,1)} %get-tuple-element.117), channel_id=1, source_target_pairs={{0,1},{1,2},{2,3},{3,4},{4,5},{5,6},{6,7},{7,8},{8,9},{9,10},{10,1... | collective-permute-start | bytes 884744 | tf_op jit(solution)/shard_map/while/body/eval_jaxpr/ppermute | solution.py:10
  57.0 10.7 %collective-permute-start = (bf16[128,1152]{1,0:T(8,128)(2,1)}, bf16[128,1152]{1,0:T(8,128)(2,1)S(1)}, u32[]{:S(2)}, u32[]{:S(2)}) collective-permute-start(bf16[128,1152]{1,0:T(8,128)(2,1)} %get-tuple-element.116), channel_id=1, source_target_pairs={{0,1},{1,2},{2,3},{3,4},{4,5},{5,6},{6,7},{7,8},{8,9},{9,10},{10,1... | collective-permute-start | bytes 884744 | tf_op jit(solution)/shard_map/while/body/eval_jaxpr/ppermute | solution.py:10
  61.0 8.3 %collective-permute-start.1 = (bf16[128,1152]{1,0:T(8,128)(2,1)}, bf16[128,1152]{1,0:T(8,128)(2,1)S(1)}, u32[]{:S(2)}, u32[]{:S(2)}) collective-permute-start(bf16[128,1152]{1,0:T(8,128)(2,1)} %get-tuple-element.117), channel_id=1, source_target_pairs={{0,1},{1,2},{2,3},{3,4},{4,5},{5,6},{6,7},{7,8},{8,9},{9,10},{10,1... | collective-permute-start | bytes 884744 | tf_op jit(solution)/shard_map/while/body/eval_jaxpr/ppermute | solution.py:10
  70.6 11.6 %collective-permute-start = (bf16[128,1152]{1,0:T(8,128)(2,1)}, bf16[128,1152]{1,0:T(8,128)(2,1)S(1)}, u32[]{:S(2)}, u32[]{:S(2)}) collective-permute-start(bf16[128,1152]{1,0:T(8,128)(2,1)} %get-tuple-element.116), channel_id=1, source_target_pairs={{0,1},{1,2},{2,3},{3,4},{4,5},{5,6},{6,7},{7,8},{8,9},{9,10},{10,1... | collective-permute-start | bytes 884744 | tf_op jit(solution)/shard_map/while/body/eval_jaxpr/ppermute | solution.py:10
  73.3 10.4 %collective-permute-start.1 = (bf16[128,1152]{1,0:T(8,128)(2,1)}, bf16[128,1152]{1,0:T(8,128)(2,1)S(1)}, u32[]{:S(2)}, u32[]{:S(2)}) collective-permute-start(bf16[128,1152]{1,0:T(8,128)(2,1)} %get-tuple-element.117), channel_id=1, source_target_pairs={{0,1},{1,2},{2,3},{3,4},{4,5},{5,6},{6,7},{7,8},{8,9},{9,10},{10,1... | collective-permute-start | bytes 884744 | tf_op jit(solution)/shard_map/while/body/eval_jaxpr/ppermute | solution.py:10
  85.0 11.6 %collective-permute-start = (bf16[128,1152]{1,0:T(8,128)(2,1)}, bf16[128,1152]{1,0:T(8,128)(2,1)S(1)}, u32[]{:S(2)}, u32[]{:S(2)}) collective-permute-start(bf16[128,1152]{1,0:T(8,128)(2,1)} %get-tuple-element.116), channel_id=1, source_target_pairs={{0,1},{1,2},{2,3},{3,4},{4,5},{5,6},{6,7},{7,8},{8,9},{9,10},{10,1... | collective-permute-start | bytes 884744 | tf_op jit(solution)/shard_map/while/body/eval_jaxpr/ppermute | solution.py:10
  85.6 12.6 %collective-permute-start.1 = (bf16[128,1152]{1,0:T(8,128)(2,1)}, bf16[128,1152]{1,0:T(8,128)(2,1)S(1)}, u32[]{:S(2)}, u32[]{:S(2)}) collective-permute-start(bf16[128,1152]{1,0:T(8,128)(2,1)} %get-tuple-element.117), channel_id=1, source_target_pairs={{0,1},{1,2},{2,3},{3,4},{4,5},{5,6},{6,7},{7,8},{8,9},{9,10},{10,1... | collective-permute-start | bytes 884744 | tf_op jit(solution)/shard_map/while/body/eval_jaxpr/ppermute | solution.py:10
  99.4 11.6 %collective-permute-start = (bf16[128,1152]{1,0:T(8,128)(2,1)}, bf16[128,1152]{1,0:T(8,128)(2,1)S(1)}, u32[]{:S(2)}, u32[]{:S(2)}) collective-permute-start(bf16[128,1152]{1,0:T(8,128)(2,1)} %get-tuple-element.116), channel_id=1, source_target_pairs={{0,1},{1,2},{2,3},{3,4},{4,5},{5,6},{6,7},{7,8},{8,9},{9,10},{10,1... | collective-permute-start | bytes 884744 | tf_op jit(solution)/shard_map/while/body/eval_jaxpr/ppermute | solution.py:10
  99.5 13.1 %collective-permute-start.1 = (bf16[128,1152]{1,0:T(8,128)(2,1)}, bf16[128,1152]{1,0:T(8,128)(2,1)S(1)}, u32[]{:S(2)}, u32[]{:S(2)}) collective-permute-start(bf16[128,1152]{1,0:T(8,128)(2,1)} %get-tuple-element.117), channel_id=1, source_target_pairs={{0,1},{1,2},{2,3},{3,4},{4,5},{5,6},{6,7},{7,8},{8,9},{9,10},{10,1... | collective-permute-start | bytes 884744 | tf_op jit(solution)/shard_map/while/body/eval_jaxpr/ppermute | solution.py:10
  113.9 11.6 %collective-permute-start = (bf16[128,1152]{1,0:T(8,128)(2,1)}, bf16[128,1152]{1,0:T(8,128)(2,1)S(1)}, u32[]{:S(2)}, u32[]{:S(2)}) collective-permute-start(bf16[128,1152]{1,0:T(8,128)(2,1)} %get-tuple-element.116), channel_id=1, source_target_pairs={{0,1},{1,2},{2,3},{3,4},{4,5},{5,6},{6,7},{7,8},{8,9},{9,10},{10,1... | collective-permute-start | bytes 884744 | tf_op jit(solution)/shard_map/while/body/eval_jaxpr/ppermute | solution.py:10
  114.0 13.1 %collective-permute-start.1 = (bf16[128,1152]{1,0:T(8,128)(2,1)}, bf16[128,1152]{1,0:T(8,128)(2,1)S(1)}, u32[]{:S(2)}, u32[]{:S(2)}) collective-permute-start(bf16[128,1152]{1,0:T(8,128)(2,1)} %get-tuple-element.117), channel_id=1, source_target_pairs={{0,1},{1,2},{2,3},{3,4},{4,5},{5,6},{6,7},{7,8},{8,9},{9,10},{10,1... | collective-permute-start | bytes 884744 | tf_op jit(solution)/shard_map/while/body/eval_jaxpr/ppermute | solution.py:10
  128.3 11.6 %collective-permute-start = (bf16[128,1152]{1,0:T(8,128)(2,1)}, bf16[128,1152]{1,0:T(8,128)(2,1)S(1)}, u32[]{:S(2)}, u32[]{:S(2)}) collective-permute-start(bf16[128,1152]{1,0:T(8,128)(2,1)} %get-tuple-element.116), channel_id=1, source_target_pairs={{0,1},{1,2},{2,3},{3,4},{4,5},{5,6},{6,7},{7,8},{8,9},{9,10},{10,1... | collective-permute-start | bytes 884744 | tf_op jit(solution)/shard_map/while/body/eval_jaxpr/ppermute | solution.py:10
  128.4 13.1 %collective-permute-start.1 = (bf16[128,1152]{1,0:T(8,128)(2,1)}, bf16[128,1152]{1,0:T(8,128)(2,1)S(1)}, u32[]{:S(2)}, u32[]{:S(2)}) collective-permute-start(bf16[128,1152]{1,0:T(8,128)(2,1)} %get-tuple-element.117), channel_id=1, source_target_pairs={{0,1},{1,2},{2,3},{3,4},{4,5},{5,6},{6,7},{7,8},{8,9},{9,10},{10,1... | collective-permute-start | bytes 884744 | tf_op jit(solution)/shard_map/while/body/eval_jaxpr/ppermute | solution.py:10
  142.8 11.6 %collective-permute-start = (bf16[128,1152]{1,0:T(8,128)(2,1)}, bf16[128,1152]{1,0:T(8,128)(2,1)S(1)}, u32[]{:S(2)}, u32[]{:S(2)}) collective-permute-start(bf16[128,1152]{1,0:T(8,128)(2,1)} %get-tuple-element.116), channel_id=1, source_target_pairs={{0,1},{1,2},{2,3},{3,4},{4,5},{5,6},{6,7},{7,8},{8,9},{9,10},{10,1... | collective-permute-start | bytes 884744 | tf_op jit(solution)/shard_map/while/body/eval_jaxpr/ppermute | solution.py:10
  142.9 13.1 %collective-permute-start.1 = (bf16[128,1152]{1,0:T(8,128)(2,1)}, bf16[128,1152]{1,0:T(8,128)(2,1)S(1)}, u32[]{:S(2)}, u32[]{:S(2)}) collective-permute-start(bf16[128,1152]{1,0:T(8,128)(2,1)} %get-tuple-element.117), channel_id=1, source_target_pairs={{0,1},{1,2},{2,3},{3,4},{4,5},{5,6},{6,7},{7,8},{8,9},{9,10},{10,1... | collective-permute-start | bytes 884744 | tf_op jit(solution)/shard_map/while/body/eval_jaxpr/ppermute | solution.py:10
  157.2 11.6 %collective-permute-start = (bf16[128,1152]{1,0:T(8,128)(2,1)}, bf16[128,1152]{1,0:T(8,128)(2,1)S(1)}, u32[]{:S(2)}, u32[]{:S(2)}) collective-permute-start(bf16[128,1152]{1,0:T(8,128)(2,1)} %get-tuple-element.116), channel_id=1, source_target_pairs={{0,1},{1,2},{2,3},{3,4},{4,5},{5,6},{6,7},{7,8},{8,9},{9,10},{10,1... | collective-permute-start | bytes 884744 | tf_op jit(solution)/shard_map/while/body/eval_jaxpr/ppermute | solution.py:10
  157.3 13.1 %collective-permute-start.1 = (bf16[128,1152]{1,0:T(8,128)(2,1)}, bf16[128,1152]{1,0:T(8,128)(2,1)S(1)}, u32[]{:S(2)}, u32[]{:S(2)}) collective-permute-start(bf16[128,1152]{1,0:T(8,128)(2,1)} %get-tuple-element.117), channel_id=1, source_target_pairs={{0,1},{1,2},{2,3},{3,4},{4,5},{5,6},{6,7},{7,8},{8,9},{9,10},{10,1... | collective-permute-start | bytes 884744 | tf_op jit(solution)/shard_map/while/body/eval_jaxpr/ppermute | solution.py:10
  171.7 11.6 %collective-permute-start = (bf16[128,1152]{1,0:T(8,128)(2,1)}, bf16[128,1152]{1,0:T(8,128)(2,1)S(1)}, u32[]{:S(2)}, u32[]{:S(2)}) collective-permute-start(bf16[128,1152]{1,0:T(8,128)(2,1)} %get-tuple-element.116), channel_id=1, source_target_pairs={{0,1},{1,2},{2,3},{3,4},{4,5},{5,6},{6,7},{7,8},{8,9},{9,10},{10,1... | collective-permute-start | bytes 884744 | tf_op jit(solution)/shard_map/while/body/eval_jaxpr/ppermute | solution.py:10
  171.7 13.1 %collective-permute-start.1 = (bf16[128,1152]{1,0:T(8,128)(2,1)}, bf16[128,1152]{1,0:T(8,128)(2,1)S(1)}, u32[]{:S(2)}, u32[]{:S(2)}) collective-permute-start(bf16[128,1152]{1,0:T(8,128)(2,1)} %get-tuple-element.117), channel_id=1, source_target_pairs={{0,1},{1,2},{2,3},{3,4},{4,5},{5,6},{6,7},{7,8},{8,9},{9,10},{10,1... | collective-permute-start | bytes 884744 | tf_op jit(solution)/shard_map/while/body/eval_jaxpr/ppermute | solution.py:10
  186.1 11.6 %collective-permute-start = (bf16[128,1152]{1,0:T(8,128)(2,1)}, bf16[128,1152]{1,0:T(8,128)(2,1)S(1)}, u32[]{:S(2)}, u32[]{:S(2)}) collective-permute-start(bf16[128,1152]{1,0:T(8,128)(2,1)} %get-tuple-element.116), channel_id=1, source_target_pairs={{0,1},{1,2},{2,3},{3,4},{4,5},{5,6},{6,7},{7,8},{8,9},{9,10},{10,1... | collective-permute-start | bytes 884744 | tf_op jit(solution)/shard_map/while/body/eval_jaxpr/ppermute | solution.py:10
  186.2 13.1 %collective-permute-start.1 = (bf16[128,1152]{1,0:T(8,128)(2,1)}, bf16[128,1152]{1,0:T(8,128)(2,1)S(1)}, u32[]{:S(2)}, u32[]{:S(2)}) collective-permute-start(bf16[128,1152]{1,0:T(8,128)(2,1)} %get-tuple-element.117), channel_id=1, source_target_pairs={{0,1},{1,2},{2,3},{3,4},{4,5},{5,6},{6,7},{7,8},{8,9},{9,10},{10,1... | collective-permute-start | bytes 884744 | tf_op jit(solution)/shard_map/while/body/eval_jaxpr/ppermute | solution.py:10
  200.5 11.6 %collective-permute-start = (bf16[128,1152]{1,0:T(8,128)(2,1)}, bf16[128,1152]{1,0:T(8,128)(2,1)S(1)}, u32[]{:S(2)}, u32[]{:S(2)}) collective-permute-start(bf16[128,1152]{1,0:T(8,128)(2,1)} %get-tuple-element.116), channel_id=1, source_target_pairs={{0,1},{1,2},{2,3},{3,4},{4,5},{5,6},{6,7},{7,8},{8,9},{9,10},{10,1... | collective-permute-start | bytes 884744 | tf_op jit(solution)/shard_map/while/body/eval_jaxpr/ppermute | solution.py:10
  200.6 13.1 %collective-permute-start.1 = (bf16[128,1152]{1,0:T(8,128)(2,1)}, bf16[128,1152]{1,0:T(8,128)(2,1)S(1)}, u32[]{:S(2)}, u32[]{:S(2)}) collective-permute-start(bf16[128,1152]{1,0:T(8,128)(2,1)} %get-tuple-element.117), channel_id=1, source_target_pairs={{0,1},{1,2},{2,3},{3,4},{4,5},{5,6},{6,7},{7,8},{8,9},{9,10},{10,1... | collective-permute-start | bytes 884744 | tf_op jit(solution)/shard_map/while/body/eval_jaxpr/ppermute | solution.py:10
  215.0 11.6 %collective-permute-start = (bf16[128,1152]{1,0:T(8,128)(2,1)}, bf16[128,1152]{1,0:T(8,128)(2,1)S(1)}, u32[]{:S(2)}, u32[]{:S(2)}) collective-permute-start(bf16[128,1152]{1,0:T(8,128)(2,1)} %get-tuple-element.116), channel_id=1, source_target_pairs={{0,1},{1,2},{2,3},{3,4},{4,5},{5,6},{6,7},{7,8},{8,9},{9,10},{10,1... | collective-permute-start | bytes 884744 | tf_op jit(solution)/shard_map/while/body/eval_jaxpr/ppermute | solution.py:10
  215.1 13.1 %collective-permute-start.1 = (bf16[128,1152]{1,0:T(8,128)(2,1)}, bf16[128,1152]{1,0:T(8,128)(2,1)S(1)}, u32[]{:S(2)}, u32[]{:S(2)}) collective-permute-start(bf16[128,1152]{1,0:T(8,128)(2,1)} %get-tuple-element.117), channel_id=1, source_target_pairs={{0,1},{1,2},{2,3},{3,4},{4,5},{5,6},{6,7},{7,8},{8,9},{9,10},{10,1... | collective-permute-start | bytes 884744 | tf_op jit(solution)/shard_map/while/body/eval_jaxpr/ppermute | solution.py:10
  229.4 11.6 %collective-permute-start.2 = (bf16[128,1152]{1,0:T(8,128)(2,1)}, bf16[128,1152]{1,0:T(8,128)(2,1)S(1)}, u32[]{:S(2)}, u32[]{:S(2)}) collective-permute-start(bf16[128,1152]{1,0:T(8,128)(2,1)} %get-tuple-element.41), channel_id=1, source_target_pairs={{0,1},{1,2},{2,3},{3,4},{4,5},{5,6},{6,7},{7,8},{8,9},{9,10},{10,1... | collective-permute-start | bytes 884744 | tf_op jit(solution)/shard_map/ppermute | solution.py:10
  241.2 124.2 %copy-start.2 = (u32[256]{0:T(256)S(1)}, u32[256]{0:T(256)}, u32[]{:S(2)}) copy-start(u32[256]{0:T(256)} %constant.19) | copy-start | bytes 3076
  241.2 125.5 %copy-start.4 = (u32[256]{0:T(256)S(1)}, u32[256]{0:T(256)}, u32[]{:S(2)}) copy-start(u32[256]{0:T(256)} %constant.23) | copy-start | bytes 3076
  359.6 8.4 %collective-permute-start.3 = (bf16[45,1152]{1,0:T(8,128)(2,1)S(1)}, bf16[45,1152]{1,0:T(8,128)(2,1)S(1)}, u32[]{:S(2)}, u32[]{:S(2)}) collective-permute-start(bf16[45,1152]{1,0:T(8,128)(2,1)S(1)} %slice), channel_id=1, source_target_pairs={{0,1},{1,2},{2,3},{3,4},{4,5},{5,6},{6,7},{7,8},{8,9},{9,10},{10,1... | collective-permute-start | bytes 311048
Sparse Core Ops, SparseCore 0:
  371.6 125.4 all-reduce.4
where the time goes:
time: 515 us; the launch traced here: 506 us
  waiting for transfers between devices  279 us (54%)
  blocking collectives  113 us (22%)
  matrix products  46.5 us (9%)
  starting transfers between devices  29.7 us (6%)
  between operations  16.8 us (3%)
  local copies, waits for them, and re-layouts  16.2 us (3%)
    ppermute x31, waiting for transfers between devices, shifted(): return lax.ppermute(value, axis, pairs)  154 us
    unnamed x3, waiting for transfers between devices  124 us
    unnamed x1, blocking collectives  113 us
    ppermute x31, starting transfers between devices, shifted(): return lax.ppermute(value, axis, pairs)  23.8 us
    dot_general x17, matrix products, contract_first(): lax.dot_general(weight, values, (((0,), (0,)), ((), ())), preferred_eleme...  21.3 us
    dot_general x16, matrix products, pair_weights(): lax.dot_general(left_units, right_units, (((1,), (1,)), ((), ())), prefer...  14.9 us
    while x15, local copies, waits for them, and re-layouts  10.7 us
  transfers between devices with their start and end apart: 33, of which 20 were waited for; matrix products, arithmetic and copies ran while one was open for 5% of the time, Pallas kernels for 0%

commit v1 on v0

v1 whole, which is shorter than its diff:
```python
import functools

import jax
import jax.numpy as jnp
from jax import lax
from jax.experimental import pallas as pl
from jax.experimental.pallas import tpu as pltpu
from jax.sharding import PartitionSpec as P

MESH = pl.DeviceIdType.MESH
BF16 = jnp.bfloat16
F32 = jnp.float32

ROWS = 128
D = 1152
FF = 4304
FF_DEV = 269
FF_PAD = 272
D_DEV = 72
HALF = 640
CHUNK = 512
HALF_ROWS = ROWS // 2
N_SENDS = 19


def nt_dot(left, right):
    return lax.dot_general(left, right, (((1,), (1,)), ((), ())), preferred_element_type=F32)


class Place:
    def __init__(self):
        self.g = lax.axis_index("grp")
        self.b = lax.axis_index("blk")
        y, rest = lax.div(self.b, 4), lax.rem(self.b, 4)
        xh, self.c = lax.div(rest, 2), lax.rem(rest, 2)

        def at(dy, flip_x, flip_c):
            x = 1 - xh if flip_x else xh
            c = 1 - self.c if flip_c else self.c
            return lax.rem(y + dy, 4) * 4 + x * 2 + c

        self.at = at
        self.chip = lambda dy, flip_x: lax.rem(y + dy, 4) * 2 + (1 - xh if flip_x else xh)
        self.xl, self.z = lax.div(self.g, 8), lax.rem(self.g, 8)


FULL, LOW, HIGH = (0, ROWS), (0, HALF_ROWS), (HALF_ROWS, HALF_ROWS)
UP, DOWN, ACROSS, TWIN = (1, 0, 0), (3, 0, 0), (0, 1, 0), (0, 0, 1)
SENDS = [
    ((0, 0, 0), FULL, ACROSS, (0, 1, 0)),
    ((0, 0, 0), FULL, UP, (3, 0, 0)),
    ((0, 0, 0), FULL, DOWN, (1, 0, 0)),
    ((3, 0, 0), LOW, UP, (2, 0, 0)),
    ((1, 0, 0), HIGH, DOWN, (2, 0, 0)),
    ((0, 1, 0), FULL, UP, (3, 1, 0)),
    ((0, 1, 0), FULL, DOWN, (1, 1, 0)),
    ((3, 1, 0), LOW, UP, (2, 1, 0)),
    ((1, 1, 0), HIGH, DOWN, (2, 1, 0)),
    ((0, 0, 0), FULL, TWIN, (0, 0, 1)),
    ((0, 1, 0), FULL, TWIN, (0, 1, 1)),
    ((3, 0, 0), FULL, TWIN, (3, 0, 1)),
    ((1, 0, 0), FULL, TWIN, (1, 0, 1)),
    ((3, 1, 0), FULL, TWIN, (3, 1, 1)),
    ((1, 1, 0), FULL, TWIN, (1, 1, 1)),
    ((2, 0, 0), LOW, TWIN, (2, 0, 1)),
    ((2, 0, 0), HIGH, TWIN, (2, 0, 1)),
    ((2, 1, 0), LOW, TWIN, (2, 1, 1)),
    ((2, 1, 0), HIGH, TWIN, (2, 1, 1)),
]


class Gather:
    def __init__(self, place, buf, send_sem, recv_sem):
        self.place, self.buf, self.send_sem, self.recv_sem = place, buf, send_sem, recv_sem
        self.held = []

    def copy(self, i, block):
        _, (first, count), target, _ = SENDS[i]
        ref = self.buf.at[self.place.at(*block), pl.ds(first, count)]
        return pltpu.make_async_remote_copy(
            src_ref=ref,
            dst_ref=ref,
            send_sem=self.send_sem.at[i],
            recv_sem=self.recv_sem.at[i],
            device_id=(self.place.g, self.place.at(*target)),
            device_id_type=MESH,
        )

    def send(self, *which):
        for i in which:
            copy = self.copy(i, SENDS[i][0])
            copy.start()
            self.held.append(copy)

    def got(self, *which):
        for i in which:
            self.copy(i, SENDS[i][3]).wait_recv()

    def start(self):
        self.send(0, 1, 2, 9)

    def stage_a(self):
        self.got(1)
        self.send(3, 11)
        self.got(2)
        self.send(4, 12)

    def stage_b(self):
        self.got(0)
        self.send(5, 6, 10)

    def stage_c(self):
        self.got(3)
        self.send(15)
        self.got(4)
        self.send(16)

    def stage_d(self):
        self.got(5)
        self.send(7, 13)
        self.got(6)
        self.send(8, 14)

    def stage_e(self):
        self.got(7)
        self.send(17)
        self.got(8)
        self.send(18)

    def finish(self):
        for copy in self.held:
            copy.wait_send()


ORDER = [
    ((0, 0), (9,)),
    ((3, 0), (11,)),
    ((1, 0), (12,)),
    ((0, 1), (10,)),
    ((2, 0), (15, 16)),
    ((3, 1), (13,)),
    ((1, 1), (14,)),
    ((2, 1), (17, 18)),
]


def kernel(
    image_ref, hidden_ref, weight_ref, positive_ref, scale_ref, bias_ref,
    image_out, head_out,
    weight_buf, images, texts, grads, raw, text_sum, image_sum,
    piece_out, piece_in, head, head_half, half_in, part_out, part_in,
    weight_sem, img_send, img_recv, txt_send, txt_recv, grd_send, grd_recv,
    hid_send, hid_recv, half_sem, part_send, part_recv,
):
    place = Place()
    g, b, c, xl, z = place.g, place.b, place.c, place.xl, place.z

    barrier = pltpu.get_barrier_semaphore()
    for d in range(1, 16):
        pl.semaphore_signal(barrier, inc=1, device_id=(g, lax.rem(b + d, 16)), device_id_type=MESH)
    other_half = (1 - xl) * 8 + z
    pl.semaphore_signal(barrier, inc=1, device_id=(other_half, b), device_id_type=MESH)
    for d in range(1, 8):
        peer = xl * 8 + lax.rem(z + d, 8)
        pl.semaphore_signal(barrier, inc=1, device_id=(peer, b), device_id_type=MESH)

    bounds = [(k, min(CHUNK, FF - k)) for k in range(0, FF, CHUNK)]
    weight_copies = []
    for n, (first, count) in enumerate(bounds):
        rows = pl.ds(first, count)
        copy = pltpu.make_async_copy(weight_ref.at[rows], weight_buf.at[rows], weight_sem.at[n])
        copy.start()
        weight_copies.append(copy)

    def unit_of(values):
        norm = jnp.sqrt(jnp.sum(values * values, axis=-1, keepdims=True) + 1e-06)
        return norm, values / norm

    def unit_back(values, incoming):
        norm, direction = unit_of(values)
        along = jnp.sum(direction * incoming, axis=-1, keepdims=True)
        return (incoming - direction * along) / norm

    images[b] = unit_of(image_ref[...].astype(F32))[1].astype(BF16)
    pl.semaphore_wait(barrier, 23)

    img = Gather(place, images, img_send, img_recv)
    txt = Gather(place, texts, txt_send, txt_recv)
    grd = Gather(place, grads, grd_send, grd_recv)
    img.start()

    between = {3: img.stage_a, 5: img.stage_b, 6: img.stage_c, 8: img.stage_d}
    for n, (first, count) in enumerate(bounds):
        weight_copies[n].wait()
        term = jnp.dot(
            hidden_ref[:, first : first + count],
            weight_buf[first : first + count],
            preferred_element_type=F32,
        )
        raw[...] = term if n == 0 else raw[...] + term
        if n in between:
            between[n]()
    texts[b] = unit_of(raw[...])[1].astype(BF16)

    def cut(first, window, shift):
        row = lax.broadcasted_iota(jnp.int32, (FF_PAD, window), 0)
        column = lax.broadcasted_iota(jnp.int32, (FF_PAD, window), 1)
        pick = jnp.where(column == row + shift, 1.0, 0.0).astype(BF16)
        return nt_dot(pick, hidden_ref[:, pl.ds(first, window)]).astype(BF16)

    def cut_step(n, carry):
        start = n * FF_DEV
        first = pl.multiple_of(lax.div(start, 128) * 128, 128)
        piece_out[n] = cut(first, 512, start - first)
        return carry

    lax.fori_loop(0, 15, cut_step, 0)
    last = 15 * FF_DEV
    piece_out[15] = cut(last // 128 * 128, FF - last // 128 * 128, last % 128)
    img.stage_e()

    pair, lane = lax.div(b, 2), pl.multiple_of(c * 128, 128)
    piece_in[pair, :, pl.ds(lane, 128)] = piece_out[b]

    def piece_copy(d, target, sender):
        return pltpu.make_async_remote_copy(
            src_ref=piece_out.at[target],
            dst_ref=piece_in.at[lax.div(sender, 2), :, pl.ds(pl.multiple_of(lax.rem(sender, 2) * 128, 128), 128)],
            send_sem=hid_send.at[d - 1],
            recv_sem=hid_recv.at[d - 1],
            device_id=(g, target),
            device_id_type=MESH,
        )

    for d in range(1, 16):
        piece_copy(d, lax.rem(b + d, 16), b).start()

    logit_scale = jnp.exp(scale_ref[...])
    logit_bias = bias_ref[...]
    text_row = lax.broadcasted_iota(jnp.int32, (ROWS, ROWS), 0)
    label = jnp.where(text_row == positive_ref[...], 1.0, 0.0)

    def with_twin(own):
        return jnp.concatenate([jnp.where(c == 0, own, 0.0), jnp.where(c == 0, 0.0, own)], axis=1)

    def visit(unit, others, chip, total, own_label=None):
        block = others[pl.ds(2 * chip, 2)].reshape(2 * ROWS, D)
        chance = jax.nn.sigmoid(logit_scale * nt_dot(unit, block) + logit_bias)
        if own_label is not None:
            chance = chance - with_twin(own_label)
        weight = (logit_scale * chance).astype(BF16)
        term = jnp.dot(weight, block, preferred_element_type=F32)
        total[...] = term if own_label is not None else total[...] + term

    for n, (where, twins) in enumerate(ORDER):
        img.got(*twins)
        visit(texts[b], images, place.chip(*where), text_sum, label if n == 0 else None)

    grads[b] = unit_back(raw[...], text_sum[...]).astype(BF16)
    grd.start()

    for d in range(1, 16):
        piece_copy(d, lax.rem(b + d, 16), lax.rem(b + 16 - d, 16)).wait_recv()

    def add_head(n):
        where, twins = ORDER[n]
        grd.got(*twins)
        chip = place.chip(*where)
        block = grads[pl.ds(2 * chip, 2)].reshape(2 * ROWS, D)
        term = jnp.dot(piece_in[chip], block, preferred_element_type=F32)
        head[...] = term if n == 0 else head[...] + term

    add_head(0)
    grd.stage_a()
    grd.stage_b()
    add_head(1)
    add_head(2)
    grd.stage_c()
    grd.stage_d()
    add_head(3)
    add_head(4)
    txt.start()
    grd.stage_e()
    add_head(5)
    add_head(6)
    add_head(7)

    head_half[...] = head[:, pl.ds(pl.multiple_of((1 - xl) * 512, 128), HALF)].astype(BF16)
    half_copy = pltpu.make_async_remote_copy(
        src_ref=head_half,
        dst_ref=half_in,
        send_sem=half_sem.at[0],
        recv_sem=half_sem.at[1],
        device_id=(other_half, b),
        device_id_type=MESH,
    )
    half_copy.start()
    txt.stage_a()
    txt.got(9)
    visit(images[b], texts, place.chip(0, 0), image_sum, jnp.transpose(label))
    half_copy.wait_recv()
    mine = head[:, pl.ds(pl.multiple_of(xl * 512, 128), HALF)] + half_in[...].astype(F32)
    head[:, 0:HALF] = mine
    row = lax.broadcasted_iota(jnp.int32, (256, 128), 0)
    column = lax.broadcasted_iota(jnp.int32, (256, 128), 1)
    for n in range(8):
        first = n * D_DEV // 128 * 128
        shift = n * D_DEV % 128
        pick = jnp.where((row == column + shift + 64 * xl) & (column < D_DEV), 1.0, 0.0).astype(BF16)
        part_out[n] = jnp.dot(
            head[:, first : first + 256].astype(BF16), pick, preferred_element_type=F32
        ).astype(BF16)

    def part_copy(d):
        target = lax.rem(z + d, 8)
        return pltpu.make_async_remote_copy(
            src_ref=part_out.at[target],
            dst_ref=part_in.at[d - 1],
            send_sem=part_send.at[d - 1],
            recv_sem=part_recv.at[d - 1],
            device_id=(xl * 8 + target, b),
            device_id_type=MESH,
        )

    for d in range(1, 8):
        part_copy(d).start()

    txt.stage_b()
    txt.stage_c()
    txt.stage_d()
    for n in range(1, 5):
        where, twins = ORDER[n]
        txt.got(*twins)
        visit(images[b], texts, place.chip(*where), image_sum)
    txt.stage_e()
    for n in range(5, 8):
        where, twins = ORDER[n]
        txt.got(*twins)
        visit(images[b], texts, place.chip(*where), image_sum)
    image_out[...] = unit_back(image_ref[...].astype(F32), image_sum[...])

    total = part_out[z].astype(F32)
    for d in range(1, 8):
        part_copy(d).wait_recv()
        total = total + part_in[d - 1].astype(F32)
    head_out[...] = total[:FF_DEV, :D_DEV]

    img.finish()
    txt.finish()
    grd.finish()
    for d in range(1, 16):
        piece_copy(d, lax.rem(b + d, 16), b).wait_send()
    for d in range(1, 8):
        part_copy(d).wait_send()
    half_copy.wait_send()


def local(image_emb, text_hidden, head_weight, positive, log_scale, bias):
    vmem = pl.BlockSpec(memory_space=pltpu.VMEM)
    dma = pltpu.SemaphoreType.DMA
    return pl.pallas_call(
        kernel,
        out_shape=(
            jax.ShapeDtypeStruct((ROWS, D), F32),
            jax.ShapeDtypeStruct((FF_DEV, D_DEV), F32),
        ),
        in_specs=[vmem, vmem, pl.BlockSpec(memory_space=pl.ANY), vmem, vmem, vmem],
        out_specs=(vmem, vmem),
        scratch_shapes=[
            pltpu.VMEM((FF, D), BF16),
            pltpu.VMEM((16, ROWS, D), BF16),
            pltpu.VMEM((16, ROWS, D), BF16),
            pltpu.VMEM((16, ROWS, D), BF16),
            pltpu.VMEM((ROWS, D), F32),
            pltpu.VMEM((ROWS, D), F32),
            pltpu.VMEM((ROWS, D), F32),
            pltpu.VMEM((16, FF_PAD, ROWS), BF16),
            pltpu.VMEM((8, FF_PAD, 2 * ROWS), BF16),
            pltpu.VMEM((FF_PAD, D), F32),
            pltpu.VMEM((FF_PAD, HALF), BF16),
            pltpu.VMEM((FF_PAD, HALF), BF16),
            pltpu.VMEM((8, FF_PAD, 128), BF16),
            pltpu.VMEM((7, FF_PAD, 128), BF16),
            dma((9,)),
            dma((N_SENDS,)),
            dma((N_SENDS,)),
            dma((N_SENDS,)),
            dma((N_SENDS,)),
            dma((N_SENDS,)),
            dma((N_SENDS,)),
            dma((15,)),
            dma((15,)),
            dma((2,)),
            dma((7,)),
            dma((7,)),
        ],
        compiler_params=pltpu.CompilerParams(
            collective_id=0, has_side_effects=True, vmem_limit_bytes=60 * 1024 * 1024
        ),
    )(
        image_emb,
        text_hidden,
        head_weight,
        positive,
        log_scale.reshape(1, 1),
        bias.reshape(1, 1),
    )


def solution(mesh):
    in_specs = (
        P(("grp", "blk"), None),
        P(("grp", "blk"), None),
        P(),
        P(("grp", "blk"), None),
        P(),
        P(),
    )
    out_specs = (P(("grp", "blk"), None), P("blk", "grp"))
    return jax.shard_map(local, mesh=mesh, in_specs=in_specs, out_specs=out_specs, check_vma=False)
```

time: 515 us -> 110 us (0.21); the launches traced: 506 us -> 110 us
  waiting for transfers between devices: 279 us -> 0 us
  blocking collectives: 113 us -> 0 us
  Pallas kernels: 0 us -> 102 us
  matrix products: 46.5 us -> 0 us
  starting transfers between devices: 29.7 us -> 0 us
  between operations: 16.8 us -> 1.93 us
  local copies, waits for them, and re-layouts: 16.2 us -> 5.96 us
    ppermute x31 -> x0, waiting for transfers between devices: 154 us -> none  [shifted(): return lax.ppermute(value, axis, pairs)]
    unnamed x3 -> x0, waiting for transfers between devices: 124 us -> none
    unnamed x1 -> x0, blocking collectives: 113 us -> none
    pallas_call x0 -> x1, Pallas kernels: none -> 102 us  [local(): pl.pallas_call(kernel, out_shape=(jax.ShapeDtypeStruct((ROWS, D), F32), j...]
    dot_general x50 -> x0, matrix products: 46.5 us -> none  [the longest x17 21.3 us: contract_first(): lax.dot_general(weight, values, (((0,), (0,)), ((), ())), preferred_eleme...]
    ppermute x31 -> x0, starting transfers between devices: 23.8 us -> none  [shifted(): return lax.ppermute(value, axis, pairs)]
    while x15 -> x0, local copies, waits for them, and re-layouts: 10.7 us -> none
    unnamed x2 -> x0, starting transfers between devices: 5.91 us -> none
  transfers between devices with their start and end apart: 33 -> 0, of which waited for: 20 -> 0; matrix products, arithmetic and copies ran while one was open for 5% -> 0% of each run, Pallas kernels for 0% -> 0%
where the time goes in v1:
time: 110 us
  Pallas kernels  102 us (93%)
  local copies, waits for them, and re-layouts  5.96 us (5%)
  between operations  1.93 us (2%)
    pallas_call x1, Pallas kernels, local(): pl.pallas_call(kernel, out_shape=(jax.ShapeDtypeStruct((ROWS, D), F32), j...  102 us
    unnamed x2, local copies, waits for them, and re-layouts  4.29 us

profile of v1, /device:TPU:1, one launch (start us, length us, event | category | flops | bytes accessed | tf_op | source)
XLA Modules:
  0.0 109.7 jit_solution(9810800937968691621)
XLA Ops:
  1.9 2.4 %copy.8.hidden_ref = bf16[128,4304]{1,0:T(8,128)(2,1)} copy(bf16[128,4304]{0,1:T(8,128)(2,1)} %param.7) | data formatting | bytes 2203648 | tf_op args[1]
  4.3 101.8 %shard_map.77 = (f32[128,1152]{1,0:T(8,128)}, f32[269,72]{1,0:T(8,128)}) custom-call(bf16[128,1152]{1,0:T(8,128)(2,1)} %image_ref.1, bf16[128,4304]{1,0:T(8,128)(2,1)} %copy.8.hidden_ref, bf16[4304,1152]{1,0:T(8,128)(2,1)} %weight_ref.1, s32[1,128]{1,0:T(1,128)} %positive_ref.1, f32[1,1]{1,0:T(1,128)} %bitcast.2.scale_ref, f32[1,1]{1,0:T(1,128)} %bitcast.3.bias_ref), custom_call_target="tpu_custom_call" | custom-call | tf_op jit(solution)/shard_map/pallas_call | solution.py:361
  106.1 1.7 %copy.9 = f32[269,72]{0,1:T(8,128)} copy(f32[269,72]{1,0:T(8,128)} %get-tuple-element.3) | data formatting | bytes 154944 | tf_op jit(solution)/shard_map/pallas_call | solution.py:361
  107.8 1.9 %copy.13 = f32[128,1152]{1,0:T(8,128)} copy(f32[128,1152]{1,0:T(8,128)} %get-tuple-element.6) | data formatting | bytes 1179648

commit v2 on v0

v2 whole, which is shorter than its diff:
```python
import jax
import jax.numpy as jnp
from jax import lax
from jax.experimental import pallas as pl
from jax.experimental.pallas import tpu as pltpu
from jax.sharding import PartitionSpec as P

MESH = pl.DeviceIdType.MESH
BF16 = jnp.bfloat16
F32 = jnp.float32

ROWS = 128
D = 1152
FF = 4304
FF_DEV = 269
FF_PAD = 272
WINDOW = 288
D_DEV = 72
LANES = 640
CHUNK = 512
FIRST_ROWS = 128


def nt_dot(left, right):
    return lax.dot_general(left, right, (((1,), (1,)), ((), ())), preferred_element_type=F32)


def tn_dot(left, right):
    return lax.dot_general(left, right, (((0,), (0,)), ((), ())), preferred_element_type=F32)


class Place:
    def __init__(self):
        self.g = lax.axis_index("grp")
        self.b = lax.axis_index("blk")
        rest = lax.rem(self.b, 4)
        self.y, self.xh, self.c = lax.div(self.b, 4), lax.div(rest, 2), lax.rem(rest, 2)
        self.xl, self.z = lax.div(self.g, 8), lax.rem(self.g, 8)

    def slot(self, dy, flip_c):
        return self.turn(dy) * 2 + (1 - self.c if flip_c else self.c)

    def turn(self, dy):
        return lax.rem(self.y + dy, 4)

    def device(self, dy=0, flip_c=0, flip_xh=0, flip_xl=0, dz=0):
        c = 1 - self.c if flip_c else self.c
        xh = 1 - self.xh if flip_xh else self.xh
        xl = 1 - self.xl if flip_xl else self.xl
        return (xl * 8 + lax.rem(self.z + dz, 8), self.turn(dy) * 4 + xh * 2 + c)


FULL, LOW, HIGH = (0, ROWS), (0, ROWS // 2), (ROWS // 2, ROWS // 2)
OWN, UP, DOWN, FAR, TWIN = (0, 0), (1, 0), (3, 0), (2, 0), (0, 1)
SENDS = [
    (OWN, LOW, UP, DOWN),
    (OWN, HIGH, DOWN, UP),
    (OWN, HIGH, UP, DOWN),
    (OWN, LOW, DOWN, UP),
    (DOWN, LOW, UP, FAR),
    (UP, HIGH, DOWN, FAR),
    (OWN, FULL, TWIN, TWIN),
    (DOWN, FULL, TWIN, (3, 1)),
    (UP, FULL, TWIN, (1, 1)),
    (FAR, LOW, TWIN, (2, 1)),
    (FAR, HIGH, TWIN, (2, 1)),
]
ORDER = [(0, (6,)), (3, (7,)), (1, (8,)), (2, (9, 10))]


class Gather:
    def __init__(self, place, buf, send_sem, recv_sem):
        self.place, self.buf, self.send_sem, self.recv_sem = place, buf, send_sem, recv_sem
        self.held = []

    def copy(self, i, block):
        _, (first, count), target, _ = SENDS[i]
        ref = self.buf.at[self.place.slot(*block), pl.ds(first, count)]
        return pltpu.make_async_remote_copy(
            src_ref=ref,
            dst_ref=ref,
            send_sem=self.send_sem.at[i],
            recv_sem=self.recv_sem.at[i],
            device_id=self.place.device(*target),
            device_id_type=MESH,
        )

    def send(self, *which):
        for i in which:
            copy = self.copy(i, SENDS[i][0])
            copy.start()
            self.held.append(copy)

    def got(self, *which):
        for i in which:
            self.copy(i, SENDS[i][3]).wait_recv()

    def start(self):
        self.send(0, 1, 2, 3, 6)

    def pass_on(self):
        self.got(0)
        self.send(4)
        self.got(1)
        self.send(5)

    def near(self):
        self.got(2)
        self.send(7)
        self.got(3)
        self.send(8)

    def far(self):
        self.got(4)
        self.send(9)
        self.got(5)
        self.send(10)

    def finish(self):
        for copy in self.held:
            copy.wait_send()


def kernel(
    image_ref, hidden_ref, weight_ref, positive_ref, scale_ref, bias_ref,
    image_out, head_out,
    weight_buf, images, texts, grads, image_far, text_far, raw,
    text_sum, image_sum, far_sum, text_back_out, text_back_in, image_back_out, image_back_in,
    piece_out, piece_in, head, head_out16, head_in, turned, part_a, part_b, in_a, in_b,
    weight_sem, img_send, img_recv, txt_send, txt_recv, grd_send, grd_recv,
    x_send, x_recv, hid_send, hid_recv, half_send, half_recv, part_send, part_recv,
):
    place = Place()
    y, c, xh, xl, z = place.y, place.c, place.xh, place.xl, place.z
    own = place.slot(*OWN)

    barrier = pltpu.get_barrier_semaphore()
    peers = [place.device(dy, fc) for dy in range(4) for fc in range(2) if dy or fc]
    peers += [place.device(flip_xh=1), place.device(flip_xl=1), place.device(flip_xh=1, flip_xl=1)]
    peers += [place.device(dz=d) for d in range(1, 8)]
    for peer in peers:
        pl.semaphore_signal(barrier, inc=1, device_id=peer, device_id_type=MESH)

    bounds = [(k, min(CHUNK, FF - k)) for k in range(0, FF, CHUNK)]
    weight_copies = []
    for n, (first, count) in enumerate(bounds):
        rows = pl.ds(first, count)
        copy = pltpu.make_async_copy(weight_ref.at[rows], weight_buf.at[rows], weight_sem.at[n])
        copy.start()
        weight_copies.append(copy)

    def unit_of(values):
        norm = jnp.sqrt(jnp.sum(values * values, axis=-1, keepdims=True) + 1e-06)
        return norm, values / norm

    def unit_back(values, incoming):
        norm, direction = unit_of(values)
        along = jnp.sum(direction * incoming, axis=-1, keepdims=True)
        return (incoming - direction * along) / norm

    def across(n, src, dst):
        return pltpu.make_async_remote_copy(
            src_ref=src,
            dst_ref=dst,
            send_sem=x_send.at[n],
            recv_sem=x_recv.at[n],
            device_id=place.device(flip_xh=1),
            device_id_type=MESH,
        )

    img = Gather(place, images, img_send, img_recv)
    txt = Gather(place, texts, txt_send, txt_recv)
    grd = Gather(place, grads, grd_send, grd_recv)
    image_across = across(0, images.at[own], image_far)
    text_across = across(1, texts.at[own], text_far)
    text_back = across(2, text_back_out, text_back_in)
    image_back = across(3, image_back_out, image_back_in)

    def begin():
        images[own] = unit_of(image_ref[...].astype(F32))[1].astype(BF16)
        pl.semaphore_wait(barrier, len(peers))
        img.start()
        image_across.start()

    between = {1: begin, 8: img.pass_on}
    for n, (first, count) in enumerate(bounds):
        weight_copies[n].wait()
        rows = pl.ds(first, count)
        term = tn_dot(hidden_ref[rows], weight_buf[rows])
        raw[...] = term if n == 0 else raw[...] + term
        if n in between:
            between[n]()
    texts[own] = unit_of(raw[...])[1].astype(BF16)
    text_across.start()
    img.near()

    def cut(start, first, window):
        row = lax.broadcasted_iota(jnp.int32, (FF_PAD, window), 0)
        column = lax.broadcasted_iota(jnp.int32, (FF_PAD, window), 1)
        pick = jnp.where(column == row + (start - first), 1.0, 0.0).astype(BF16)
        return jnp.dot(
            pick, hidden_ref[pl.ds(first, window)], preferred_element_type=F32
        ).astype(BF16)

    def cut_step(n, carry):
        start = n * FF_DEV
        first = pl.multiple_of(lax.div(start, 16) * 16, 16)
        column, half = lax.div(n, 4) * 2 + lax.rem(n, 2), lax.rem(lax.div(n, 2), 2)
        rows = pl.ds(pl.multiple_of(half * FF_PAD, 16), FF_PAD)
        piece_out[column, rows] = cut(start, first, WINDOW)
        return carry

    lax.fori_loop(0, 15, cut_step, 0)
    last = 15 * FF_DEV
    piece_out[7, FF_PAD : 2 * FF_PAD] = cut(last, last // 16 * 16, FF - last // 16 * 16)

    def lane(core):
        return pl.ds(pl.multiple_of(core * ROWS, ROWS), ROWS)

    OTHERS = [(dy, fc) for dy in (1, 3, 2) for fc in range(2)] + [TWIN]

    def piece_copy(n, dy, fc, back=False):
        if back:
            dst = piece_in.at[place.turn(4 - dy), :, lane(1 - c if fc else c)]
        else:
            dst = piece_in.at[y, :, lane(c)]
        return pltpu.make_async_remote_copy(
            src_ref=piece_out.at[place.slot(dy, fc)],
            dst_ref=dst,
            send_sem=hid_send.at[n],
            recv_sem=hid_recv.at[n],
            device_id=place.device(dy, fc),
            device_id_type=MESH,
        )

    pieces = [piece_copy(n, *target) for n, target in enumerate(OTHERS)]
    for copy in pieces:
        copy.start()
    piece_in[y, :, lane(c)] = piece_out[own]
    img.far()

    logit_scale = jnp.exp(scale_ref[...])
    logit_bias = bias_ref[...]
    text_row = lax.broadcasted_iota(jnp.int32, (ROWS, ROWS), 0)
    label = jnp.where(text_row == positive_ref[...], 1.0, 0.0)

    def with_twin(value):
        return jnp.concatenate(
            [jnp.where(c == 0, value, 0.0), jnp.where(c == 0, 0.0, value)], axis=1
        )

    def chip(buf, dy):
        return buf[pl.ds(2 * place.turn(dy), 2)].reshape(2 * ROWS, D)

    def visit(unit, block, total, first, own_label=None):
        chance = jax.nn.sigmoid(logit_scale * nt_dot(unit, block) + logit_bias)
        if own_label is not None:
            chance = chance - with_twin(own_label)
        weight = (logit_scale * chance).astype(BF16)
        term = jnp.dot(weight, block, preferred_element_type=F32)
        total[...] = term if first else total[...] + term

    for n, (dy, twins) in enumerate(ORDER):
        img.got(*twins)
        visit(texts[own], chip(images, dy), text_sum, n == 0, label if n == 0 else None)
    text_across.wait_recv()
    for n, (dy, _) in enumerate(ORDER):
        visit(text_far[...], chip(images, dy), far_sum, n == 0)
    text_back_out[...] = far_sum[...].astype(BF16)
    text_back.start()
    for n, (dy, fc) in enumerate(OTHERS):
        piece_copy(n, dy, fc, back=True).wait_recv()
    text_back.wait_recv()
    incoming = text_sum[...] + text_back_in[...].astype(F32)
    grads[own] = unit_back(raw[...], incoming).astype(BF16)
    grd.start()

    def add_head(dy, n):
        term = jnp.dot(piece_in[place.turn(dy)], chip(grads, dy), preferred_element_type=F32)
        head[...] = term if n == 0 else head[...] + term

    grd.got(6)
    add_head(0, 0)
    grd.pass_on()
    txt.start()
    grd.near()
    grd.got(7)
    add_head(3, 1)
    grd.got(8)
    add_head(1, 2)
    grd.far()
    grd.got(9, 10)
    add_head(2, 3)
    head_out16[...] = head[...].astype(BF16)

    PARTS = [(0, FIRST_ROWS), (FIRST_ROWS, FF_PAD - FIRST_ROWS)]
    FLIPS = [(0, 1), (1, 0), (1, 1)]

    def half_copy(n, flips, part):
        flip_xh, flip_xl = flips
        first, count = PARTS[part]
        to_xh = 1 - xh if flip_xh else xh
        to_xl = 1 - xl if flip_xl else xl
        rows = pl.ds(pl.multiple_of(to_xh * FF_PAD + first, 16), count)
        lanes = pl.ds(pl.multiple_of(to_xl * 512, 128), LANES)
        return pltpu.make_async_remote_copy(
            src_ref=head_out16.at[rows, lanes],
            dst_ref=head_in.at[n, pl.ds(first, count)],
            send_sem=half_send.at[part * 3 + n],
            recv_sem=half_recv.at[part * 3 + n],
            device_id=place.device(flip_xh=flip_xh, flip_xl=flip_xl),
            device_id_type=MESH,
        )

    halves = [[half_copy(n, flips, part) for n, flips in enumerate(FLIPS)] for part in range(2)]
    for copy in halves[0]:
        copy.start()
    txt.pass_on()
    for copy in halves[0]:
        copy.wait_send()
    for copy in halves[1]:
        copy.start()
    txt.near()

    def summed(part):
        first, count = PARTS[part]
        for copy in halves[part]:
            copy.wait_recv()
        rows = pl.ds(pl.multiple_of(xh * FF_PAD + first, 16), count)
        total = head[rows, pl.ds(pl.multiple_of(xl * 512, 128), LANES)]
        for n in range(3):
            total = total + head_in[n, first : first + count].astype(F32)
        return total

    def turned_rows(n):
        return pl.ds(pl.multiple_of(n * D_DEV + xl * 64, 8), D_DEV)

    def part_copy(d, part):
        target = lax.rem(z + d, 8)
        src, dst = ((part_a, in_a), (part_b, in_b))[part]
        return pltpu.make_async_remote_copy(
            src_ref=src.at[target],
            dst_ref=dst.at[d - 1],
            send_sem=part_send.at[part * 7 + d - 1],
            recv_sem=part_recv.at[part * 7 + d - 1],
            device_id=place.device(dz=d),
            device_id_type=MESH,
        )

    ROUND = (1, 7, 2, 6, 3, 5, 4)
    parts = [[part_copy(d, part) for d in ROUND] for part in range(2)]

    turned[...] = jnp.transpose(summed(0))
    for n in range(8):
        part_a[n, 0:D_DEV] = turned[turned_rows(n)].astype(BF16)
    for copy in parts[0]:
        copy.start()

    txt.got(6)
    visit(images[own], chip(texts, 0), image_sum, True, jnp.transpose(label))
    total = summed(1)
    turned[...] = jnp.transpose(total[0:128])
    row = lax.broadcasted_iota(jnp.int32, (256, 128), 0)
    column = lax.broadcasted_iota(jnp.int32, (256, 128), 1)
    rest = total[128:144].astype(BF16)
    for n in range(8):
        part_b[n, 0:D_DEV] = turned[turned_rows(n)].astype(BF16)
        first = min(n * D_DEV // 128 * 128, LANES - 256)
        shift = n * D_DEV - first + 64 * xl
        pick = jnp.where((row == column + shift) & (column < D_DEV), 1.0, 0.0).astype(BF16)
        part_b[n, 80:96] = jnp.dot(
            rest[:, first : first + 256], pick, preferred_element_type=F32
        ).astype(BF16)
    for copy in parts[1]:
        copy.start()

    txt.far()
    txt.got(7, 8, 9, 10)
    image_across.wait_recv()
    for n, (dy, _) in enumerate(ORDER):
        visit(image_far[...], chip(texts, dy), far_sum, n == 0)
    image_back_out[...] = far_sum[...].astype(BF16)
    image_back.start()
    for n, (dy, _) in enumerate(ORDER):
        if n:
            visit(images[own], chip(texts, dy), image_sum, False)

    def gathered(part, mine, count):
        total = mine[z].astype(F32)
        landed = (in_a, in_b)[part]
        for copy in parts[part]:
            copy.wait_recv()
        for n in range(7):
            total = total + landed[n].astype(F32)
        return total

    head_out[:, 0:128] = gathered(0, part_a, 80)[0:D_DEV]
    total = gathered(1, part_b, 96)
    head_out[:, 128:256] = total[0:D_DEV]
    tail = jnp.concatenate([total[80:96], jnp.zeros((112, 128), F32)], axis=0)
    head_out[:, 256:FF_DEV] = jnp.transpose(tail)[0:D_DEV, 0 : FF_DEV - 256]

    image_back.wait_recv()
    incoming = image_sum[...] + image_back_in[...].astype(F32)
    image_out[...] = unit_back(image_ref[...].astype(F32), incoming)

    img.finish()
    txt.finish()
    grd.finish()
    for copy in pieces + halves[1] + parts[0] + parts[1]:
        copy.wait_send()
    for copy in (image_across, text_across, text_back, image_back):
        copy.wait_send()


def local(image_emb, text_hidden, head_weight, positive, log_scale, bias):
    vmem = pl.BlockSpec(memory_space=pltpu.VMEM)
    dma = pltpu.SemaphoreType.DMA
    sends = len(SENDS)
    image_grad, head_turned = pl.pallas_call(
        kernel,
        out_shape=(
            jax.ShapeDtypeStruct((ROWS, D), F32),
            jax.ShapeDtypeStruct((D_DEV, FF_DEV), F32),
        ),
        in_specs=[vmem, vmem, pl.BlockSpec(memory_space=pl.ANY), vmem, vmem, vmem],
        out_specs=(vmem, vmem),
        scratch_shapes=[
            pltpu.VMEM((FF, D), BF16),
            pltpu.VMEM((8, ROWS, D), BF16),
            pltpu.VMEM((8, ROWS, D), BF16),
            pltpu.VMEM((8, ROWS, D), BF16),
            pltpu.VMEM((ROWS, D), BF16),
            pltpu.VMEM((ROWS, D), BF16),
            pltpu.VMEM((ROWS, D), F32),
            pltpu.VMEM((ROWS, D), F32),
            pltpu.VMEM((ROWS, D), F32),
            pltpu.VMEM((ROWS, D), F32),
            pltpu.VMEM((ROWS, D), BF16),
            pltpu.VMEM((ROWS, D), BF16),
            pltpu.VMEM((ROWS, D), BF16),
            pltpu.VMEM((ROWS, D), BF16),
            pltpu.VMEM((8, 2 * FF_PAD, ROWS), BF16),
            pltpu.VMEM((4, 2 * FF_PAD, 2 * ROWS), BF16),
            pltpu.VMEM((2 * FF_PAD, D), F32),
            pltpu.VMEM((2 * FF_PAD, D), BF16),
            pltpu.VMEM((3, FF_PAD, LANES), BF16),
            pltpu.VMEM((LANES, 128), F32),
            pltpu.VMEM((8, 80, 128), BF16),
            pltpu.VMEM((8, 96, 128), BF16),
            pltpu.VMEM((7, 80, 128), BF16),
            pltpu.VMEM((7, 96, 128), BF16),
            dma((9,)),
            dma((sends,)),
            dma((sends,)),
            dma((sends,)),
            dma((sends,)),
            dma((sends,)),
            dma((sends,)),
            dma((4,)),
            dma((4,)),
            dma((7,)),
            dma((7,)),
            dma((6,)),
            dma((6,)),
            dma((14,)),
            dma((14,)),
        ],
        compiler_params=pltpu.CompilerParams(
            collective_id=0, has_side_effects=True, vmem_limit_bytes=60 * 1024 * 1024
        ),
    )(
        image_emb,
        text_hidden.T,
        head_weight,
        positive,
        log_scale.reshape(1, 1),
        bias.reshape(1, 1),
    )
    return image_grad, head_turned.T


def solution(mesh):
    in_specs = (
        P(("grp", "blk"), None),
        P(("grp", "blk"), None),
        P(),
        P(("grp", "blk"), None),
        P(),
        P(),
    )
    out_specs = (P(("grp", "blk"), None), P("blk", "grp"))
    return jax.shard_map(local, mesh=mesh, in_specs=in_specs, out_specs=out_specs, check_vma=False)
```

time: 515 us -> 92.4 us (0.18); the launches traced: 506 us -> 92.2 us
  waiting for transfers between devices: 279 us -> 0 us
  blocking collectives: 113 us -> 0 us
  Pallas kernels: 0 us -> 86.8 us
  matrix products: 46.5 us -> 0 us
  starting transfers between devices: 29.7 us -> 0 us
  between operations: 16.8 us -> 1.93 us
  local copies, waits for them, and re-layouts: 16.2 us -> 3.47 us
    ppermute x31 -> x0, waiting for transfers between devices: 154 us -> none  [shifted(): return lax.ppermute(value, axis, pairs)]
    unnamed x3 -> x0, waiting for transfers between devices: 124 us -> none
    unnamed x1 -> x0, blocking collectives: 113 us -> none
    pallas_call x0 -> x1, Pallas kernels: none -> 86.8 us  [local(): pl.pallas_call(kernel, out_shape=(jax.ShapeDtypeStruct((ROWS, D), F32), j...]
    dot_general x50 -> x0, matrix products: 46.5 us -> none  [the longest x17 21.3 us: contract_first(): lax.dot_general(weight, values, (((0,), (0,)), ((), ())), preferred_eleme...]
    ppermute x31 -> x0, starting transfers between devices: 23.8 us -> none  [shifted(): return lax.ppermute(value, axis, pairs)]
    while x15 -> x0, local copies, waits for them, and re-layouts: 10.7 us -> none
    unnamed x2 -> x0, starting transfers between devices: 5.91 us -> none
  transfers between devices with their start and end apart: 33 -> 0, of which waited for: 20 -> 0; matrix products, arithmetic and copies ran while one was open for 5% -> 0% of each run, Pallas kernels for 0% -> 0%
where the time goes in v2:
time: 92.4 us; the launch traced here: 92.2 us
  Pallas kernels  86.8 us (94%)
  local copies, waits for them, and re-layouts  3.47 us (4%)
  between operations  1.93 us (2%)
    pallas_call x1, Pallas kernels, local(): pl.pallas_call(kernel, out_shape=(jax.ShapeDtypeStruct((ROWS, D), F32), j...  86.8 us
    unnamed x2, local copies, waits for them, and re-layouts  3.47 us

profile of v2, /device:TPU:1, one launch (start us, length us, event | category | flops | bytes accessed | tf_op | source)
XLA Modules:
  0.0 92.2 jit_solution(10844296468153701578)
XLA Ops:
  1.9 86.8 %shard_map.77 = (f32[128,1152]{1,0:T(8,128)}, f32[72,269]{1,0:T(8,128)}) custom-call(bf16[128,1152]{1,0:T(8,128)(2,1)} %image_ref.1, bf16[4304,128]{1,0:T(8,128)(2,1)} %bitcast.6, bf16[4304,1152]{1,0:T(8,128)(2,1)} %weight_ref.1, s32[1,128]{1,0:T(1,128)} %positive_ref.1, f32[1,1]{1,0:T(1,128)} %bitcast.4.scale_ref, f32[1,1]{1,0:T(1,128)} %bitcast.5.bias_ref), custom_call_target="tpu_custom_call" | custom-call | tf_op jit(solution)/shard_map/pallas_call | solution.py:420
  88.7 1.9 %copy.12 = f32[128,1152]{1,0:T(8,128)} copy(f32[128,1152]{1,0:T(8,128)} %get-tuple-element.8) | data formatting | bytes 1179648
  90.6 1.5 %copy.13 = f32[269,72]{0,1:T(8,128)} copy(f32[269,72]{0,1:T(8,128)} %bitcast.7) | data formatting | bytes 154944

commit v3 on v2

v3 whole, which is shorter than its diff:
```python
import jax
import jax.numpy as jnp
from jax import lax
from jax.experimental import pallas as pl
from jax.experimental.pallas import tpu as pltpu
from jax.sharding import PartitionSpec as P

MESH = pl.DeviceIdType.MESH
BF16 = jnp.bfloat16
F32 = jnp.float32

ROWS = 128
D = 1152
FF = 4304
FF_DEV = 269
FF_PAD = 272
WINDOW = 288
D_DEV = 72
LANES = 640
CHUNK = 512
A_ROWS, B_ROWS = 144, 128


def nt_dot(left, right):
    return lax.dot_general(left, right, (((1,), (1,)), ((), ())), preferred_element_type=F32)


def tn_dot(left, right):
    return lax.dot_general(left, right, (((0,), (0,)), ((), ())), preferred_element_type=F32)


class Place:
    def __init__(self):
        self.g = lax.axis_index("grp")
        self.b = lax.axis_index("blk")
        rest = lax.rem(self.b, 4)
        self.y, self.xh, self.c = lax.div(self.b, 4), lax.div(rest, 2), lax.rem(rest, 2)
        self.xl, self.z = lax.div(self.g, 8), lax.rem(self.g, 8)

    def slot(self, dy, flip_c):
        return self.turn(dy) * 2 + (1 - self.c if flip_c else self.c)

    def turn(self, dy):
        return lax.rem(self.y + dy, 4)

    def device(self, dy=0, flip_c=0, flip_xh=0, flip_xl=0, dz=0):
        c = 1 - self.c if flip_c else self.c
        xh = 1 - self.xh if flip_xh else self.xh
        xl = 1 - self.xl if flip_xl else self.xl
        return (xl * 8 + lax.rem(self.z + dz, 8), self.turn(dy) * 4 + xh * 2 + c)


FULL, LOW, HIGH = (0, ROWS), (0, ROWS // 2), (ROWS // 2, ROWS // 2)
OWN, UP, DOWN, FAR, TWIN = (0, 0), (1, 0), (3, 0), (2, 0), (0, 1)
SENDS = [
    (OWN, LOW, UP, DOWN),
    (OWN, HIGH, DOWN, UP),
    (OWN, HIGH, UP, DOWN),
    (OWN, LOW, DOWN, UP),
    (DOWN, LOW, UP, FAR),
    (UP, HIGH, DOWN, FAR),
    (OWN, FULL, TWIN, TWIN),
    (DOWN, FULL, TWIN, (3, 1)),
    (UP, FULL, TWIN, (1, 1)),
    (FAR, LOW, TWIN, (2, 1)),
    (FAR, HIGH, TWIN, (2, 1)),
]
ORDER = [(0, (6,)), (3, (7,)), (1, (8,)), (2, (9, 10))]


class Gather:
    def __init__(self, place, buf, send_sem, recv_sem):
        self.place, self.buf, self.send_sem, self.recv_sem = place, buf, send_sem, recv_sem
        self.held = []

    def copy(self, i, block):
        _, (first, count), target, _ = SENDS[i]
        ref = self.buf.at[self.place.slot(*block), pl.ds(first, count)]
        return pltpu.make_async_remote_copy(
            src_ref=ref,
            dst_ref=ref,
            send_sem=self.send_sem.at[i],
            recv_sem=self.recv_sem.at[i],
            device_id=self.place.device(*target),
            device_id_type=MESH,
        )

    def send(self, *which):
        for i in which:
            copy = self.copy(i, SENDS[i][0])
            copy.start()
            self.held.append(copy)

    def got(self, *which):
        for i in which:
            self.copy(i, SENDS[i][3]).wait_recv()

    def pass_on(self):
        self.got(0)
        self.send(4)
        self.got(1)
        self.send(5)

    def near(self):
        self.got(2)
        self.send(7)
        self.got(3)
        self.send(8)

    def far(self):
        self.got(4)
        self.send(9)
        self.got(5)
        self.send(10)

    def finish(self):
        for copy in self.held:
            copy.wait_send()


def kernel(
    image_ref, hidden_ref, weight_ref, positive_ref, scale_ref, bias_ref,
    image_out, head_out,
    weight_buf, images, texts, far_texts, grads, raw,
    text_sum, image_sum, far_sum, text_back_out, text_back_in,
    piece_out, piece_in, head, head_a, head_in, turned, turned_b,
    part_a, part_b, in_a, in_b, sum_b, far_b,
    weight_sem, img_send, img_recv, txt_send, txt_recv, far_send, far_recv, grd_send, grd_recv,
    x_send, x_recv, hid_send, hid_recv, half_send, half_recv, part_send, part_recv,
):
    place = Place()
    y, c, xh, xl, z = place.y, place.c, place.xh, place.xl, place.z
    own = place.slot(*OWN)

    barrier = pltpu.get_barrier_semaphore()
    peers = [place.device(dy, fc) for dy in range(4) for fc in range(2) if dy or fc]
    peers += [place.device(flip_xh=1), place.device(flip_xl=1), place.device(flip_xh=1, flip_xl=1)]
    peers += [place.device(dz=d) for d in range(1, 8)]
    for peer in peers:
        pl.semaphore_signal(barrier, inc=1, device_id=peer, device_id_type=MESH)

    bounds = [(k, min(CHUNK, FF - k)) for k in range(0, FF, CHUNK)]
    weight_copies = []
    for n, (first, count) in enumerate(bounds):
        rows = pl.ds(first, count)
        copy = pltpu.make_async_copy(weight_ref.at[rows], weight_buf.at[rows], weight_sem.at[n])
        copy.start()
        weight_copies.append(copy)

    def unit_of(values):
        norm = jnp.sqrt(jnp.sum(values * values, axis=-1, keepdims=True) + 1e-06)
        return norm, values / norm

    def unit_back(values, incoming):
        norm, direction = unit_of(values)
        along = jnp.sum(direction * incoming, axis=-1, keepdims=True)
        return (incoming - direction * along) / norm

    def remote(src, dst, send_sem, recv_sem, target):
        return pltpu.make_async_remote_copy(
            src_ref=src,
            dst_ref=dst,
            send_sem=send_sem,
            recv_sem=recv_sem,
            device_id=target,
            device_id_type=MESH,
        )

    img = Gather(place, images, img_send, img_recv)
    txt = Gather(place, texts, txt_send, txt_recv)
    far = Gather(place, far_texts, far_send, far_recv)
    grd = Gather(place, grads, grd_send, grd_recv)
    partner = place.device(flip_xh=1)
    text_across = remote(texts.at[own], far_texts.at[own], x_send.at[0], x_recv.at[0], partner)
    text_back = remote(text_back_out, text_back_in, x_send.at[1], x_recv.at[1], partner)

    def cut(start, first, window):
        row = lax.broadcasted_iota(jnp.int32, (FF_PAD, window), 0)
        column = lax.broadcasted_iota(jnp.int32, (FF_PAD, window), 1)
        wanted = jnp.where(row < 128, row, jnp.where(row < A_ROWS, row + 128, row - 16))
        pick = jnp.where(column == wanted + (start - first), 1.0, 0.0).astype(BF16)
        return jnp.dot(
            pick, hidden_ref[pl.ds(first, window)], preferred_element_type=F32
        ).astype(BF16)

    def cut_step(n, carry):
        start = n * FF_DEV
        first = pl.multiple_of(lax.div(start, 16) * 16, 16)
        column, half = lax.div(n, 4) * 2 + lax.rem(n, 2), lax.rem(lax.div(n, 2), 2)
        rows = pl.ds(pl.multiple_of(half * FF_PAD, 16), FF_PAD)
        piece_out[column, rows] = cut(start, first, WINDOW)
        return carry

    images[own] = unit_of(image_ref[...].astype(F32))[1].astype(BF16)
    lax.fori_loop(0, 5, cut_step, 0)
    pl.semaphore_wait(barrier, len(peers))
    img.send(0, 1, 2, 3, 6)
    lax.fori_loop(5, 15, cut_step, 0)
    last = 15 * FF_DEV
    piece_out[7, FF_PAD : 2 * FF_PAD] = cut(last, last // 16 * 16, FF - last // 16 * 16)

    for n, (first, count) in enumerate(bounds):
        weight_copies[n].wait()
        rows = pl.ds(first, count)
        term = tn_dot(hidden_ref[rows], weight_buf[rows])
        raw[...] = term if n == 0 else raw[...] + term
    texts[own] = unit_of(raw[...])[1].astype(BF16)
    text_across.start()
    txt.send(6)
    img.pass_on()

    def lane(core):
        return pl.ds(pl.multiple_of(core * ROWS, ROWS), ROWS)

    OTHERS = [(dy, fc) for dy in (1, 3, 2) for fc in range(2)] + [TWIN]

    def piece_copy(n, dy, fc, back=False):
        if back:
            dst = piece_in.at[place.turn(4 - dy), :, lane(1 - c if fc else c)]
        else:
            dst = piece_in.at[y, :, lane(c)]
        return remote(
            piece_out.at[place.slot(dy, fc)], dst, hid_send.at[n], hid_recv.at[n],
            place.device(dy, fc),
        )

    pieces = [piece_copy(n, *target) for n, target in enumerate(OTHERS)]
    for copy in pieces:
        copy.start()
    piece_in[y, :, lane(c)] = piece_out[own]
    img.near()

    logit_scale = jnp.exp(scale_ref[...])
    logit_bias = bias_ref[...]
    text_row = lax.broadcasted_iota(jnp.int32, (ROWS, ROWS), 0)
    label = jnp.where(text_row == positive_ref[...], 1.0, 0.0)

    def with_twin(value):
        return jnp.concatenate(
            [jnp.where(c == 0, value, 0.0), jnp.where(c == 0, 0.0, value)], axis=1
        )

    def chip(buf, dy):
        return buf[pl.ds(2 * place.turn(dy), 2)].reshape(2 * ROWS, D)

    def visit(unit, block, total, first, own_label=None):
        chance = jax.nn.sigmoid(logit_scale * nt_dot(unit, block) + logit_bias)
        if own_label is not None:
            chance = chance - with_twin(own_label)
        weight = (logit_scale * chance).astype(BF16)
        term = jnp.dot(weight, block, preferred_element_type=F32)
        total[...] = term if first else total[...] + term

    def visit_texts(n):
        label_of = label if n == 0 else None
        visit(texts[own], chip(images, ORDER[n][0]), text_sum, n == 0, label_of)

    def visit_far(n):
        visit(far_texts[own], chip(images, ORDER[n][0]), far_sum, n == 0)

    def visit_images(n, gather):
        own_label = jnp.transpose(label) if n == 0 and gather is txt else None
        block = chip(gather.buf, ORDER[n][0])
        visit(images[own], block, image_sum, own_label is not None, own_label)

    for n in range(3):
        img.got(*ORDER[n][1])
        visit_texts(n)
    img.far()
    txt.send(0, 1, 2, 3)
    text_across.wait_recv()
    far.send(6)
    for n in range(3):
        visit_far(n)
    img.got(*ORDER[3][1])
    visit_far(3)
    text_back_out[...] = far_sum[...].astype(BF16)
    text_back.start()
    visit_texts(3)
    text_back.wait_recv()
    incoming = text_sum[...] + text_back_in[...].astype(F32)
    grads[own] = unit_back(raw[...], incoming).astype(BF16)
    grd.send(0, 1, 6)
    txt.got(6)
    visit_images(0, txt)
    far.got(6)
    visit_images(0, far)
    grd.send(2, 3)
    for n, (dy, fc) in enumerate(OTHERS):
        piece_copy(n, dy, fc, back=True).wait_recv()

    def add_head(dy, n):
        term = jnp.dot(piece_in[place.turn(dy)], chip(grads, dy), preferred_element_type=F32)
        head[...] = term if n == 0 else head[...] + term

    grd.got(6)
    add_head(0, 0)
    grd.pass_on()
    grd.near()
    txt.pass_on()
    txt.near()
    grd.got(7)
    add_head(3, 1)
    grd.got(8)
    add_head(1, 2)
    grd.far()
    far.send(0, 1, 2, 3)
    grd.got(9, 10)
    add_head(2, 3)

    FLIPS = [(0, 1), (1, 0), (1, 1)]
    ROUND = (1, 7, 2, 6, 3, 5, 4)

    def window(half):
        return pl.ds(pl.multiple_of(half * 512, 128), LANES)

    def half_copy(n, flip_xh, flip_xl):
        to_xh = 1 - xh if flip_xh else xh
        to_xl = 1 - xl if flip_xl else xl
        return remote(
            head_a.at[to_xh, :, window(to_xl)], head_in.at[n], half_send.at[n], half_recv.at[n],
            place.device(flip_xh=flip_xh, flip_xl=flip_xl),
        )

    def late_copy(n, flip_xh, flip_xl):
        to_xh = 1 - xh if flip_xh else xh
        to_xl = 1 - xl if flip_xl else xl
        return remote(
            sum_b.at[2 * to_xh + to_xl], far_b.at[n], half_send.at[3 + n], half_recv.at[3 + n],
            place.device(flip_xh=flip_xh, flip_xl=flip_xl),
        )

    def part_copy(d, part):
        target = lax.rem(z + d, 8)
        src, dst = ((part_a, in_a), (part_b, in_b))[part]
        n = part * 7 + d - 1
        return remote(
            src.at[target], dst.at[d - 1], part_send.at[n], part_recv.at[n], place.device(dz=d)
        )

    halves = [half_copy(n, *flips) for n, flips in enumerate(FLIPS)]
    lates = [late_copy(n, *flips) for n, flips in enumerate(FLIPS)]
    parts = [[part_copy(d, part) for d in ROUND] for part in range(2)]

    for n in range(2):
        head_a[n] = head[n * FF_PAD : n * FF_PAD + A_ROWS].astype(BF16)
    for copy in halves:
        copy.start()
    for n in range(2):
        turned_b[...] = jnp.transpose(head[n * FF_PAD + A_ROWS : (n + 1) * FF_PAD])
        for half in range(2):
            for k in range(8):
                first = half * 8 * D_DEV + k * D_DEV
                part_b[k, 2 * n + half, 0:D_DEV] = turned_b[first : first + D_DEV].astype(BF16)
    for copy in parts[1]:
        copy.start()

    txt.far()
    for n in (1, 2):
        txt.got(*ORDER[n][1])
        visit_images(n, txt)
    far.pass_on()
    far.near()
    for n in (1, 2):
        far.got(*ORDER[n][1])
        visit_images(n, far)
    far.far()

    for copy in halves:
        copy.wait_recv()
    total = head[pl.ds(pl.multiple_of(xh * FF_PAD, 16), A_ROWS), window(xl)]
    for n in range(3):
        total = total + head_in[n].astype(F32)
    turned[...] = jnp.transpose(total[0:128])
    row = lax.broadcasted_iota(jnp.int32, (256, 128), 0)
    column = lax.broadcasted_iota(jnp.int32, (256, 128), 1)
    rest = total[128:A_ROWS].astype(BF16)
    for n in range(8):
        rows = pl.ds(pl.multiple_of(n * D_DEV + xl * 64, 8), D_DEV)
        part_a[n, 0:D_DEV] = turned[rows].astype(BF16)
        first = min(n * D_DEV // 128 * 128, LANES - 256)
        shift = n * D_DEV - first + 64 * xl
        pick = jnp.where((row == column + shift) & (column < D_DEV), 1.0, 0.0).astype(BF16)
        part_a[n, 80:96] = jnp.dot(
            rest[:, first : first + 256], pick, preferred_element_type=F32
        ).astype(BF16)
    for copy in parts[0]:
        copy.start()

    for gather in (txt, far):
        gather.got(*ORDER[3][1])
        visit_images(3, gather)
    image_out[...] = unit_back(image_ref[...].astype(F32), image_sum[...])

    for copy in parts[1]:
        copy.wait_recv()
    total = part_b[z].astype(F32)
    for n in range(7):
        total = total + in_b[n].astype(F32)
    sum_b[...] = total.astype(BF16)
    for copy in lates:
        copy.start()

    for copy in parts[0]:
        copy.wait_recv()
    total = part_a[z].astype(F32)
    for n in range(7):
        total = total + in_a[n].astype(F32)
    head_out[:, 0:128] = total[0:D_DEV]
    tail = jnp.concatenate([total[80:96], jnp.zeros((112, 128), F32)], axis=0)
    head_out[:, 256:FF_DEV] = jnp.transpose(tail)[0:D_DEV, 0 : FF_DEV - 256]
    for copy in lates:
        copy.wait_recv()
    total = sum_b[2 * xh + xl].astype(F32)
    for n in range(3):
        total = total + far_b[n].astype(F32)
    head_out[:, 128:256] = total[0:D_DEV]

    for gather in (img, txt, far, grd):
        gather.finish()
    for copy in pieces + halves + lates + parts[0] + parts[1] + [text_across, text_back]:
        copy.wait_send()


def settle(image_ref, head_ref, image_out, head_out):
    image_out[...] = image_ref[...]
    head_out[...] = head_ref[...]


def local(image_emb, text_hidden, head_weight, positive, log_scale, bias):
    vmem = pl.BlockSpec(memory_space=pltpu.VMEM)
    dma = pltpu.SemaphoreType.DMA
    sends = len(SENDS)
    image_grad, head_turned = pl.pallas_call(
        kernel,
        out_shape=(
            jax.ShapeDtypeStruct((ROWS, D), F32),
            jax.ShapeDtypeStruct((D_DEV, FF_DEV), F32),
        ),
        in_specs=[vmem, vmem, pl.BlockSpec(memory_space=pl.ANY), vmem, vmem, vmem],
        out_specs=(vmem, vmem),
        scratch_shapes=[
            pltpu.VMEM((FF, D), BF16),
            pltpu.VMEM((8, ROWS, D), BF16),
            pltpu.VMEM((8, ROWS, D), BF16),
            pltpu.VMEM((8, ROWS, D), BF16),
            pltpu.VMEM((8, ROWS, D), BF16),
            pltpu.VMEM((ROWS, D), F32),
            pltpu.VMEM((ROWS, D), F32),
            pltpu.VMEM((ROWS, D), F32),
            pltpu.VMEM((ROWS, D), F32),
            pltpu.VMEM((ROWS, D), BF16),
            pltpu.VMEM((ROWS, D), BF16),
            pltpu.VMEM((8, 2 * FF_PAD, ROWS), BF16),
            pltpu.VMEM((4, 2 * FF_PAD, 2 * ROWS), BF16),
            pltpu.VMEM((2 * FF_PAD, D), F32),
            pltpu.VMEM((2, A_ROWS, D), BF16),
            pltpu.VMEM((3, A_ROWS, LANES), BF16),
            pltpu.VMEM((LANES, 128), F32),
            pltpu.VMEM((D, 128), F32),
            pltpu.VMEM((8, 96, 128), BF16),
            pltpu.VMEM((8, 4, 80, 128), BF16),
            pltpu.VMEM((7, 96, 128), BF16),
            pltpu.VMEM((7, 4, 80, 128), BF16),
            pltpu.VMEM((4, 80, 128), BF16),
            pltpu.VMEM((3, 80, 128), BF16),
            dma((9,)),
            dma((sends,)),
            dma((sends,)),
            dma((sends,)),
            dma((sends,)),
            dma((sends,)),
            dma((sends,)),
            dma((sends,)),
            dma((sends,)),
            dma((2,)),
            dma((2,)),
            dma((7,)),
            dma((7,)),
            dma((6,)),
            dma((6,)),
            dma((14,)),
            dma((14,)),
        ],
        compiler_params=pltpu.CompilerParams(
            collective_id=0, has_side_effects=True, vmem_limit_bytes=60 * 1024 * 1024
        ),
    )(
        image_emb,
        text_hidden.T,
        head_weight,
        positive,
        log_scale.reshape(1, 1),
        bias.reshape(1, 1),
    )
    image_grad, head_turned = pl.pallas_call(
        settle,
        out_shape=(
            jax.ShapeDtypeStruct((ROWS, D), F32),
            jax.ShapeDtypeStruct((D_DEV, FF_DEV), F32),
        ),
        in_specs=[vmem, vmem],
        out_specs=(vmem, vmem),
        compiler_params=pltpu.CompilerParams(vmem_limit_bytes=60 * 1024 * 1024),
    )(image_grad, head_turned)
    return image_grad, head_turned.T


def solution(mesh):
    in_specs = (
        P(("grp", "blk"), None),
        P(("grp", "blk"), None),
        P(),
        P(("grp", "blk"), None),
        P(),
        P(),
    )
    out_specs = (P(("grp", "blk"), None), P("blk", "grp"))
    return jax.shard_map(local, mesh=mesh, in_specs=in_specs, out_specs=out_specs, check_vma=False)
```

time: 92.4 us -> 80.3 us (0.87)
  Pallas kernels: 86.8 us -> 78.2 us
  local copies, waits for them, and re-layouts: 3.47 us -> 0 us
    pallas_call x1, Pallas kernels: 86.8 us -> 76.2 us  [local(): pl.pallas_call(kernel, out_shape=(jax.ShapeDtypeStruct((ROWS, D), F32), j...]
    unnamed x2 -> x0, local copies, waits for them, and re-layouts: 3.47 us -> none
    pallas_call x0 -> x1, Pallas kernels: none -> 1.95 us  [local(): pl.pallas_call(settle, out_shape=(jax.ShapeDtypeStruct((ROWS, D), F32), j...]
where the time goes in v3:
time: 80.3 us; the launch traced here: 80.1 us
  Pallas kernels  78.2 us (97%)
  between operations  1.93 us (2%)
    pallas_call x1, Pallas kernels, local(): pl.pallas_call(kernel, out_shape=(jax.ShapeDtypeStruct((ROWS, D), F32), j...  76.2 us
    pallas_call x1, Pallas kernels, local(): pl.pallas_call(settle, out_shape=(jax.ShapeDtypeStruct((ROWS, D), F32), j...  1.95 us

profile of v3, /device:TPU:1, one launch (start us, length us, event | category | flops | bytes accessed | tf_op | source)
XLA Modules:
  0.0 80.1 jit_solution(12200244469124752444)
XLA Ops:
  1.9 76.2 %shard_map.77 = (f32[128,1152]{1,0:T(8,128)}, f32[72,269]{1,0:T(8,128)}) custom-call(bf16[128,1152]{1,0:T(8,128)(2,1)} %image_ref.1, bf16[4304,128]{1,0:T(8,128)(2,1)} %bitcast.6, bf16[4304,1152]{1,0:T(8,128)(2,1)} %weight_ref.1, s32[1,128]{1,0:T(1,128)} %positive_ref.1, f32[1,1]{1,0:T(1,128)} %bitcast.4.scale_ref, f32[1,1]{1,0:T(1,128)} %bitcast.5.bias_ref), custom_call_target="tpu_custom_call" | custom-call | tf_op jit(solution)/shard_map/pallas_call | solution.py:434
  78.2 2.0 %shard_map.78 = (f32[128,1152]{1,0:T(8,128)}, f32[72,269]{1,0:T(8,128)}) custom-call(f32[128,1152]{1,0:T(8,128)} %get-tuple-element.6.image_ref, f32[72,269]{1,0:T(8,128)} %get-tuple-element.7.head_ref), custom_call_target="tpu_custom_call" | custom-call | tf_op jit(solution)/shard_map/pallas_call | solution.py:496

commit v4 on v3

--- a/solution.py
+++ b/solution.py
@@ -225,8 +225,6 @@
         )
 
     pieces = [piece_copy(n, *target) for n, target in enumerate(OTHERS)]
-    for copy in pieces:
-        copy.start()
     piece_in[y, :, lane(c)] = piece_out[own]
     img.near()
 
@@ -267,7 +265,8 @@
         img.got(*ORDER[n][1])
         visit_texts(n)
     img.far()
-    txt.send(0, 1, 2, 3)
+    for copy in pieces:
+        copy.start()
     text_across.wait_recv()
     far.send(6)
     for n in range(3):
@@ -297,16 +296,18 @@
     add_head(0, 0)
     grd.pass_on()
     grd.near()
-    txt.pass_on()
-    txt.near()
     grd.got(7)
     add_head(3, 1)
     grd.got(8)
     add_head(1, 2)
     grd.far()
-    far.send(0, 1, 2, 3)
+    txt.send(0, 1, 2, 3)
     grd.got(9, 10)
-    add_head(2, 3)
+    last_piece, last_grads = piece_in.at[place.turn(2)], chip(grads, 2)
+
+    def add_last(rows):
+        term = jnp.dot(last_piece[rows], last_grads, preferred_element_type=F32)
+        return head[rows] + term
 
     FLIPS = [(0, 1), (1, 0), (1, 1)]
     ROUND = (1, 7, 2, 6, 3, 5, 4)
@@ -343,28 +344,28 @@
     parts = [[part_copy(d, part) for d in ROUND] for part in range(2)]
 
     for n in range(2):
-        head_a[n] = head[n * FF_PAD : n * FF_PAD + A_ROWS].astype(BF16)
-    for copy in halves:
-        copy.start()
-    for n in range(2):
-        turned_b[...] = jnp.transpose(head[n * FF_PAD + A_ROWS : (n + 1) * FF_PAD])
+        rows = pl.ds(n * FF_PAD + A_ROWS, B_ROWS)
+        turned_b[...] = jnp.transpose(add_last(rows))
         for half in range(2):
             for k in range(8):
                 first = half * 8 * D_DEV + k * D_DEV
                 part_b[k, 2 * n + half, 0:D_DEV] = turned_b[first : first + D_DEV].astype(BF16)
     for copy in parts[1]:
         copy.start()
-
-    txt.far()
+    for n in range(2):
+        rows = pl.ds(n * FF_PAD, A_ROWS)
+        total = add_last(rows)
+        head[rows] = total
+        head_a[n] = total.astype(BF16)
+    for copy in halves:
+        copy.start()
+
+    far.send(0, 1, 2, 3)
+    txt.pass_on()
+    txt.near()
     for n in (1, 2):
         txt.got(*ORDER[n][1])
         visit_images(n, txt)
-    far.pass_on()
-    far.near()
-    for n in (1, 2):
-        far.got(*ORDER[n][1])
-        visit_images(n, far)
-    far.far()
 
     for copy in halves:
         copy.wait_recv()
@@ -387,10 +388,11 @@
     for copy in parts[0]:
         copy.start()
 
-    for gather in (txt, far):
-        gather.got(*ORDER[3][1])
-        visit_images(3, gather)
-    image_out[...] = unit_back(image_ref[...].astype(F32), image_sum[...])
+    far.pass_on()
+    txt.far()
+    far.near()
+    txt.got(*ORDER[3][1])
+    visit_images(3, txt)
 
     for copy in parts[1]:
         copy.wait_recv()
@@ -400,6 +402,14 @@
     sum_b[...] = total.astype(BF16)
     for copy in lates:
         copy.start()
+
+    for n in (1, 2):
+        far.got(*ORDER[n][1])
+        visit_images(n, far)
+    far.far()
+    far.got(*ORDER[3][1])
+    visit_images(3, far)
+    image_out[...] = unit_back(image_ref[...].astype(F32), image_sum[...])
 
     for copy in parts[0]:
         copy.wait_recv()

time: 80.3 us -> 78.8 us (0.981)
  Pallas kernels: 78.2 us -> 76.7 us
    pallas_call x1, Pallas kernels: 76.2 us -> 74.8 us  [local(): pl.pallas_call(kernel, out_shape=(jax.ShapeDtypeStruct((ROWS, D), F32), j...]
where the time goes in v4:
time: 78.8 us; the launch traced here: 78.7 us
  Pallas kernels  76.7 us (97%)
  between operations  1.93 us (2%)
    pallas_call x1, Pallas kernels, local(): pl.pallas_call(kernel, out_shape=(jax.ShapeDtypeStruct((ROWS, D), F32), j...  74.8 us
    pallas_call x1, Pallas kernels, local(): pl.pallas_call(settle, out_shape=(jax.ShapeDtypeStruct((ROWS, D), F32), j...  1.95 us

profile of v4, /device:TPU:1, one launch (start us, length us, event | category | flops | bytes accessed | tf_op | source)
XLA Modules:
  0.0 78.7 jit_solution(6044102058936512778)
XLA Ops:
  1.9 74.8 %shard_map.77 = (f32[128,1152]{1,0:T(8,128)}, f32[72,269]{1,0:T(8,128)}) custom-call(bf16[128,1152]{1,0:T(8,128)(2,1)} %image_ref.1, bf16[4304,128]{1,0:T(8,128)(2,1)} %bitcast.6, bf16[4304,1152]{1,0:T(8,128)(2,1)} %weight_ref.1, s32[1,128]{1,0:T(1,128)} %positive_ref.1, f32[1,1]{1,0:T(1,128)} %bitcast.4.scale_ref, f32[1,1]{1,0:T(1,128)} %bitcast.5.bias_ref), custom_call_target="tpu_custom_call" | custom-call | tf_op jit(solution)/shard_map/pallas_call | solution.py:444
  76.7 2.0 %shard_map.78 = (f32[128,1152]{1,0:T(8,128)}, f32[72,269]{1,0:T(8,128)}) custom-call(f32[128,1152]{1,0:T(8,128)} %get-tuple-element.6.image_ref, f32[72,269]{1,0:T(8,128)} %get-tuple-element.7.head_ref), custom_call_target="tpu_custom_call" | custom-call | tf_op jit(solution)/shard_map/pallas_call | solution.py:506

commit v5 on v3

--- a/solution.py
+++ b/solution.py
@@ -19,6 +19,7 @@
 LANES = 640
 CHUNK = 512
 A_ROWS, B_ROWS = 144, 128
+LOW_LANES, HIGH_LANES = (0, LANES), (LANES, D - LANES)
 
 
 def nt_dot(left, right):
@@ -69,13 +70,14 @@
 
 
 class Gather:
-    def __init__(self, place, buf, send_sem, recv_sem):
+    def __init__(self, place, buf, send_sem, recv_sem, lanes=(0, D)):
         self.place, self.buf, self.send_sem, self.recv_sem = place, buf, send_sem, recv_sem
+        self.lanes = pl.ds(*lanes)
         self.held = []
 
     def copy(self, i, block):
         _, (first, count), target, _ = SENDS[i]
-        ref = self.buf.at[self.place.slot(*block), pl.ds(first, count)]
+        ref = self.buf.at[self.place.slot(*block), pl.ds(first, count), self.lanes]
         return pltpu.make_async_remote_copy(
             src_ref=ref,
             dst_ref=ref,
@@ -121,11 +123,12 @@
 def kernel(
     image_ref, hidden_ref, weight_ref, positive_ref, scale_ref, bias_ref,
     image_out, head_out,
-    weight_buf, images, texts, far_texts, grads, raw,
-    text_sum, image_sum, far_sum, text_back_out, text_back_in,
+    weight_buf, images, texts, far_texts, grads, raw, text_sum, image_sum, far_sum,
+    text_back_out, text_back_in,
     piece_out, piece_in, head, head_a, head_in, turned, turned_b,
     part_a, part_b, in_a, in_b, sum_b, far_b,
-    weight_sem, img_send, img_recv, txt_send, txt_recv, far_send, far_recv, grd_send, grd_recv,
+    weight_sem, img_send, img_recv, txt_send, txt_recv, far_send, far_recv,
+    low_send, low_recv, high_send, high_recv,
     x_send, x_recv, hid_send, hid_recv, half_send, half_recv, part_send, part_recv,
 ):
     place = Place()
@@ -169,10 +172,17 @@
     img = Gather(place, images, img_send, img_recv)
     txt = Gather(place, texts, txt_send, txt_recv)
     far = Gather(place, far_texts, far_send, far_recv)
-    grd = Gather(place, grads, grd_send, grd_recv)
+    grds = [
+        Gather(place, grads, low_send, low_recv, LOW_LANES),
+        Gather(place, grads, high_send, high_recv, HIGH_LANES),
+    ]
     partner = place.device(flip_xh=1)
-    text_across = remote(texts.at[own], far_texts.at[own], x_send.at[0], x_recv.at[0], partner)
-    text_back = remote(text_back_out, text_back_in, x_send.at[1], x_recv.at[1], partner)
+
+    def across(n, src, dst):
+        return remote(src, dst, x_send.at[n], x_recv.at[n], partner)
+
+    text_across = across(0, texts.at[own], far_texts.at[own])
+    text_back = across(1, text_back_out, text_back_in)
 
     def cut(start, first, window):
         row = lax.broadcasted_iota(jnp.int32, (FF_PAD, window), 0)
@@ -194,8 +204,10 @@
     images[own] = unit_of(image_ref[...].astype(F32))[1].astype(BF16)
     lax.fori_loop(0, 5, cut_step, 0)
     pl.semaphore_wait(barrier, len(peers))
-    img.send(0, 1, 2, 3, 6)
-    lax.fori_loop(5, 15, cut_step, 0)
+    img.send(0, 1, 6)
+    lax.fori_loop(5, 11, cut_step, 0)
+    img.send(2, 3)
+    lax.fori_loop(11, 15, cut_step, 0)
     last = 15 * FF_DEV
     piece_out[7, FF_PAD : 2 * FF_PAD] = cut(last, last // 16 * 16, FF - last // 16 * 16)
 
@@ -225,13 +237,13 @@
         )
 
     pieces = [piece_copy(n, *target) for n, target in enumerate(OTHERS)]
+    piece_in[y, :, lane(c)] = piece_out[own]
+    img.near()
     for copy in pieces:
         copy.start()
-    piece_in[y, :, lane(c)] = piece_out[own]
-    img.near()
-
-    logit_scale = jnp.exp(scale_ref[...])
-    logit_bias = bias_ref[...]
+
+    logit_scale = jnp.exp(jnp.full((1, 2 * ROWS), scale_ref[0], F32))
+    logit_bias = bias_ref[0]
     text_row = lax.broadcasted_iota(jnp.int32, (ROWS, ROWS), 0)
     label = jnp.where(text_row == positive_ref[...], 1.0, 0.0)
 
@@ -255,10 +267,11 @@
         label_of = label if n == 0 else None
         visit(texts[own], chip(images, ORDER[n][0]), text_sum, n == 0, label_of)
 
-    def visit_far(n):
+    def visit_far_texts(n):
         visit(far_texts[own], chip(images, ORDER[n][0]), far_sum, n == 0)
 
     def visit_images(n, gather):
+        gather.got(*ORDER[n][1])
         own_label = jnp.transpose(label) if n == 0 and gather is txt else None
         block = chip(gather.buf, ORDER[n][0])
         visit(images[own], block, image_sum, own_label is not None, own_label)
@@ -271,42 +284,41 @@
     text_across.wait_recv()
     far.send(6)
     for n in range(3):
-        visit_far(n)
+        visit_far_texts(n)
     img.got(*ORDER[3][1])
-    visit_far(3)
+    visit_far_texts(3)
     text_back_out[...] = far_sum[...].astype(BF16)
     text_back.start()
     visit_texts(3)
+    visit_images(0, txt)
+    visit_images(0, far)
     text_back.wait_recv()
     incoming = text_sum[...] + text_back_in[...].astype(F32)
     grads[own] = unit_back(raw[...], incoming).astype(BF16)
-    grd.send(0, 1, 6)
-    txt.got(6)
-    visit_images(0, txt)
-    far.got(6)
-    visit_images(0, far)
-    grd.send(2, 3)
+    grds[0].send(0, 1, 2, 3, 6)
     for n, (dy, fc) in enumerate(OTHERS):
         piece_copy(n, dy, fc, back=True).wait_recv()
 
-    def add_head(dy, n):
-        term = jnp.dot(piece_in[place.turn(dy)], chip(grads, dy), preferred_element_type=F32)
-        head[...] = term if n == 0 else head[...] + term
-
-    grd.got(6)
+    def head_term(part, n, rows):
+        first, count = (LOW_LANES, HIGH_LANES)[part]
+        lanes = pl.ds(first, count)
+        turn = place.turn(ORDER[n][0])
+        block = grads[pl.ds(2 * turn, 2), :, lanes].reshape(2 * ROWS, count)
+        term = jnp.dot(piece_in[turn, rows], block, preferred_element_type=F32)
+        return term if n == 0 else head[rows, lanes] + term
+
+    def add_head(part, n):
+        grds[part].got(*ORDER[n][1])
+        head[:, pl.ds(*(LOW_LANES, HIGH_LANES)[part])] = head_term(part, n, pl.ds(0, 2 * FF_PAD))
+
     add_head(0, 0)
-    grd.pass_on()
-    grd.near()
-    txt.pass_on()
-    txt.near()
-    grd.got(7)
-    add_head(3, 1)
-    grd.got(8)
-    add_head(1, 2)
-    grd.far()
-    far.send(0, 1, 2, 3)
-    grd.got(9, 10)
-    add_head(2, 3)
+    grds[0].pass_on()
+    grds[1].send(0, 1, 2, 3, 6)
+    grds[0].near()
+    add_head(0, 1)
+    add_head(0, 2)
+    grds[0].far()
+    grds[1].pass_on()
 
     FLIPS = [(0, 1), (1, 0), (1, 1)]
     ROUND = (1, 7, 2, 6, 3, 5, 4)
@@ -326,45 +338,65 @@
         to_xh = 1 - xh if flip_xh else xh
         to_xl = 1 - xl if flip_xl else xl
         return remote(
-            sum_b.at[2 * to_xh + to_xl], far_b.at[n], half_send.at[3 + n], half_recv.at[3 + n],
+            sum_b.at[2 * to_xl + to_xh], far_b.at[n], half_send.at[3 + n], half_recv.at[3 + n],
             place.device(flip_xh=flip_xh, flip_xl=flip_xl),
         )
 
     def part_copy(d, part):
         target = lax.rem(z + d, 8)
-        src, dst = ((part_a, in_a), (part_b, in_b))[part]
+        if part == 0:
+            src, dst = part_a.at[target], in_a.at[d - 1]
+        else:
+            pair = pl.ds(2 * (part - 1), 2)
+            src, dst = part_b.at[target, pair], in_b.at[d - 1, pair]
         n = part * 7 + d - 1
-        return remote(
-            src.at[target], dst.at[d - 1], part_send.at[n], part_recv.at[n], place.device(dz=d)
-        )
+        return remote(src, dst, part_send.at[n], part_recv.at[n], place.device(dz=d))
 
     halves = [half_copy(n, *flips) for n, flips in enumerate(FLIPS)]
     lates = [late_copy(n, *flips) for n, flips in enumerate(FLIPS)]
-    parts = [[part_copy(d, part) for d in ROUND] for part in range(2)]
-
-    for n in range(2):
-        head_a[n] = head[n * FF_PAD : n * FF_PAD + A_ROWS].astype(BF16)
-    for copy in halves:
-        copy.start()
-    for n in range(2):
-        turned_b[...] = jnp.transpose(head[n * FF_PAD + A_ROWS : (n + 1) * FF_PAD])
-        for half in range(2):
+    parts = [[part_copy(d, part) for d in ROUND] for part in range(3)]
+
+    def start_towards(copies, half):
+        for copy, (_, flip_xl) in zip(copies, FLIPS):
+            to_xl = 1 - xl if flip_xl else xl
+            pl.when(to_xl == half)(copy.start)
+
+    def send_sums(part):
+        first, count = (LOW_LANES, HIGH_LANES)[part]
+        lanes = pl.ds(first, count)
+        for n in range(2):
+            rows = pl.ds(n * FF_PAD + A_ROWS, B_ROWS)
+            turned_b[n, lanes] = jnp.transpose(head_term(part, 3, rows))
             for k in range(8):
-                first = half * 8 * D_DEV + k * D_DEV
-                part_b[k, 2 * n + half, 0:D_DEV] = turned_b[first : first + D_DEV].astype(BF16)
-    for copy in parts[1]:
-        copy.start()
-
+                begin = (8 * part + k) * D_DEV
+                part_b[k, 2 * part + n, 0:D_DEV] = turned_b[n, begin : begin + D_DEV].astype(BF16)
+        for copy in parts[1 + part]:
+            copy.start()
+        for n in range(2):
+            rows = pl.ds(n * FF_PAD, A_ROWS)
+            total = head_term(part, 3, rows)
+            head[rows, lanes] = total
+            head_a[n, :, lanes] = total.astype(BF16)
+        start_towards(halves, part)
+
+    grds[0].got(*ORDER[3][1])
+    send_sums(0)
+    grds[1].near()
+    add_head(1, 0)
+    add_head(1, 1)
+    add_head(1, 2)
+    grds[1].far()
+    far.send(0, 1, 2, 3)
+    txt.pass_on()
+    txt.near()
+    grds[1].got(*ORDER[3][1])
+    send_sums(1)
+
+    visit_images(1, txt)
+    visit_images(2, txt)
     txt.far()
-    for n in (1, 2):
-        txt.got(*ORDER[n][1])
-        visit_images(n, txt)
     far.pass_on()
-    far.near()
-    for n in (1, 2):
-        far.got(*ORDER[n][1])
-        visit_images(n, far)
-    far.far()
+    visit_images(3, txt)
 
     for copy in halves:
         copy.wait_recv()
@@ -387,19 +419,22 @@
     for copy in parts[0]:
         copy.start()
 
-    for gather in (txt, far):
-        gather.got(*ORDER[3][1])
-        visit_images(3, gather)
+    far.near()
+    for part in range(2):
+        for copy in parts[1 + part]:
+            copy.wait_recv()
+        pair = slice(2 * part, 2 * part + 2)
+        total = part_b[z, pair].astype(F32)
+        for n in range(7):
+            total = total + in_b[n, pair].astype(F32)
+        sum_b[pair] = total.astype(BF16)
+        start_towards(lates, part)
+
+    visit_images(1, far)
+    visit_images(2, far)
+    far.far()
+    visit_images(3, far)
     image_out[...] = unit_back(image_ref[...].astype(F32), image_sum[...])
-
-    for copy in parts[1]:
-        copy.wait_recv()
-    total = part_b[z].astype(F32)
-    for n in range(7):
-        total = total + in_b[n].astype(F32)
-    sum_b[...] = total.astype(BF16)
-    for copy in lates:
-        copy.start()
 
     for copy in parts[0]:
         copy.wait_recv()
@@ -411,14 +446,16 @@
     head_out[:, 256:FF_DEV] = jnp.transpose(tail)[0:D_DEV, 0 : FF_DEV - 256]
     for copy in lates:
         copy.wait_recv()
-    total = sum_b[2 * xh + xl].astype(F32)
+    total = sum_b[2 * xl + xh].astype(F32)
     for n in range(3):
         total = total + far_b[n].astype(F32)
     head_out[:, 128:256] = total[0:D_DEV]
 
-    for gather in (img, txt, far, grd):
+    for gather in (img, txt, far, *grds):
         gather.finish()
-    for copy in pieces + halves + lates + parts[0] + parts[1] + [text_across, text_back]:
+    for copy in pieces + halves + lates + parts[0] + parts[1] + parts[2]:
+        copy.wait_send()
+    for copy in (text_across, text_back):
         copy.wait_send()
 
 
@@ -429,6 +466,7 @@
 
 def local(image_emb, text_hidden, head_weight, positive, log_scale, bias):
     vmem = pl.BlockSpec(memory_space=pltpu.VMEM)
+    smem = pl.BlockSpec(memory_space=pltpu.SMEM)
     dma = pltpu.SemaphoreType.DMA
     sends = len(SENDS)
     image_grad, head_turned = pl.pallas_call(
@@ -437,7 +475,7 @@
             jax.ShapeDtypeStruct((ROWS, D), F32),
             jax.ShapeDtypeStruct((D_DEV, FF_DEV), F32),
         ),
-        in_specs=[vmem, vmem, pl.BlockSpec(memory_space=pl.ANY), vmem, vmem, vmem],
+        in_specs=[vmem, vmem, pl.BlockSpec(memory_space=pl.ANY), vmem, smem, smem],
         out_specs=(vmem, vmem),
         scratch_shapes=[
             pltpu.VMEM((FF, D), BF16),
@@ -457,7 +495,7 @@
             pltpu.VMEM((2, A_ROWS, D), BF16),
             pltpu.VMEM((3, A_ROWS, LANES), BF16),
             pltpu.VMEM((LANES, 128), F32),
-            pltpu.VMEM((D, 128), F32),
+            pltpu.VMEM((2, D, 128), F32),
             pltpu.VMEM((8, 96, 128), BF16),
             pltpu.VMEM((8, 4, 80, 128), BF16),
             pltpu.VMEM((7, 96, 128), BF16),
@@ -473,14 +511,16 @@
             dma((sends,)),
             dma((sends,)),
             dma((sends,)),
+            dma((sends,)),
+            dma((sends,)),
             dma((2,)),
             dma((2,)),
             dma((7,)),
             dma((7,)),
             dma((6,)),
             dma((6,)),
-            dma((14,)),
-            dma((14,)),
+            dma((21,)),
+            dma((21,)),
         ],
         compiler_params=pltpu.CompilerParams(
             collective_id=0, has_side_effects=True, vmem_limit_bytes=60 * 1024 * 1024
@@ -490,8 +530,8 @@
         text_hidden.T,
         head_weight,
         positive,
-        log_scale.reshape(1, 1),
-        bias.reshape(1, 1),
+        log_scale,
+        bias,
     )
     image_grad, head_turned = pl.pallas_call(
         settle,

time: 80.3 us -> 79 us (0.984)
  Pallas kernels: 78.2 us -> 76.9 us
    pallas_call x1, Pallas kernels: 76.2 us -> 74.9 us  [local(): pl.pallas_call(kernel, out_shape=(jax.ShapeDtypeStruct((ROWS, D), F32), j...]
where the time goes in v5:
time: 79 us; the launch traced here: 78.8 us
  Pallas kernels  76.9 us (97%)
  between operations  1.93 us (2%)
    pallas_call x1, Pallas kernels, local(): pl.pallas_call(kernel, out_shape=(jax.ShapeDtypeStruct((ROWS, D), F32), j...  74.9 us
    pallas_call x1, Pallas kernels, local(): pl.pallas_call(settle, out_shape=(jax.ShapeDtypeStruct((ROWS, D), F32), j...  1.95 us

profile of v5, /device:TPU:1, one launch (start us, length us, event | category | flops | bytes accessed | tf_op | source)
XLA Modules:
  0.0 78.8 jit_solution(5370119739779234038)
XLA Ops:
  1.9 74.9 %shard_map.77 = (f32[128,1152]{1,0:T(8,128)}, f32[72,269]{1,0:T(8,128)}) custom-call(bf16[128,1152]{1,0:T(8,128)(2,1)} %image_ref.1, bf16[4304,128]{1,0:T(8,128)(2,1)} %bitcast.2, bf16[4304,1152]{1,0:T(8,128)(2,1)} %weight_ref.1, s32[1,128]{1,0:T(1,128)} %positive_ref.1, f32[1]{0:T(128)S(6)} %copy.8.scale_ref, f32[1]{0:T(128)S(6)} %copy.9.bias_ref), custom_call_target="tpu_custom_call" | custom-call | tf_op jit(solution)/shard_map/pallas_call | solution.py:472
  76.9 2.0 %shard_map.78 = (f32[128,1152]{1,0:T(8,128)}, f32[72,269]{1,0:T(8,128)}) custom-call(f32[128,1152]{1,0:T(8,128)} %get-tuple-element.6.image_ref, f32[72,269]{1,0:T(8,128)} %get-tuple-element.7.head_ref), custom_call_target="tpu_custom_call" | custom-call | tf_op jit(solution)/shard_map/pallas_call | solution.py:536

commit v6 on v5

--- a/solution.py
+++ b/solution.py
@@ -123,11 +123,11 @@
 def kernel(
     image_ref, hidden_ref, weight_ref, positive_ref, scale_ref, bias_ref,
     image_out, head_out,
-    weight_buf, images, texts, far_texts, grads, raw, text_sum, image_sum, far_sum,
-    text_back_out, text_back_in,
+    weight_buf, images, texts, grads, far_image, far_text, raw, text_sum, image_sum, far_sum,
+    text_back_out, text_back_in, image_back_out, image_back_in,
     piece_out, piece_in, head, head_a, head_in, turned, turned_b,
     part_a, part_b, in_a, in_b, sum_b, far_b,
-    weight_sem, img_send, img_recv, txt_send, txt_recv, far_send, far_recv,
+    weight_sem, img_send, img_recv, txt_send, txt_recv,
     low_send, low_recv, high_send, high_recv,
     x_send, x_recv, hid_send, hid_recv, half_send, half_recv, part_send, part_recv,
 ):
@@ -171,7 +171,6 @@
 
     img = Gather(place, images, img_send, img_recv)
     txt = Gather(place, texts, txt_send, txt_recv)
-    far = Gather(place, far_texts, far_send, far_recv)
     grds = [
         Gather(place, grads, low_send, low_recv, LOW_LANES),
         Gather(place, grads, high_send, high_recv, HIGH_LANES),
@@ -181,8 +180,10 @@
     def across(n, src, dst):
         return remote(src, dst, x_send.at[n], x_recv.at[n], partner)
 
-    text_across = across(0, texts.at[own], far_texts.at[own])
+    text_across = across(0, texts.at[own], far_text)
     text_back = across(1, text_back_out, text_back_in)
+    image_across = across(2, images.at[own], far_image)
+    image_back = across(3, image_back_out, image_back_in)
 
     def cut(start, first, window):
         row = lax.broadcasted_iota(jnp.int32, (FF_PAD, window), 0)
@@ -268,13 +269,15 @@
         visit(texts[own], chip(images, ORDER[n][0]), text_sum, n == 0, label_of)
 
     def visit_far_texts(n):
-        visit(far_texts[own], chip(images, ORDER[n][0]), far_sum, n == 0)
-
-    def visit_images(n, gather):
-        gather.got(*ORDER[n][1])
-        own_label = jnp.transpose(label) if n == 0 and gather is txt else None
-        block = chip(gather.buf, ORDER[n][0])
-        visit(images[own], block, image_sum, own_label is not None, own_label)
+        visit(far_text[...], chip(images, ORDER[n][0]), far_sum, n == 0)
+
+    def visit_images(n):
+        txt.got(*ORDER[n][1])
+        own_label = jnp.transpose(label) if n == 0 else None
+        visit(images[own], chip(texts, ORDER[n][0]), image_sum, n == 0, own_label)
+
+    def visit_far_images(n):
+        visit(far_image[...], chip(texts, ORDER[n][0]), far_sum, n == 0)
 
     for n in range(3):
         img.got(*ORDER[n][1])
@@ -282,7 +285,6 @@
     img.far()
     txt.send(0, 1, 2, 3)
     text_across.wait_recv()
-    far.send(6)
     for n in range(3):
         visit_far_texts(n)
     img.got(*ORDER[3][1])
@@ -290,12 +292,12 @@
     text_back_out[...] = far_sum[...].astype(BF16)
     text_back.start()
     visit_texts(3)
-    visit_images(0, txt)
-    visit_images(0, far)
+    visit_images(0)
     text_back.wait_recv()
     incoming = text_sum[...] + text_back_in[...].astype(F32)
     grads[own] = unit_back(raw[...], incoming).astype(BF16)
     grds[0].send(0, 1, 2, 3, 6)
+    image_across.start()
     for n, (dy, fc) in enumerate(OTHERS):
         piece_copy(n, dy, fc, back=True).wait_recv()
 
@@ -381,22 +383,26 @@
 
     grds[0].got(*ORDER[3][1])
     send_sums(0)
+    image_across.wait_recv()
+    visit_far_images(0)
     grds[1].near()
     add_head(1, 0)
     add_head(1, 1)
     add_head(1, 2)
     grds[1].far()
-    far.send(0, 1, 2, 3)
     txt.pass_on()
     txt.near()
     grds[1].got(*ORDER[3][1])
     send_sums(1)
 
-    visit_images(1, txt)
-    visit_images(2, txt)
+    for n in (1, 2):
+        visit_images(n)
+        visit_far_images(n)
     txt.far()
-    far.pass_on()
-    visit_images(3, txt)
+    visit_images(3)
+    visit_far_images(3)
+    image_back_out[...] = far_sum[...].astype(BF16)
+    image_back.start()
 
     for copy in halves:
         copy.wait_recv()
@@ -419,7 +425,6 @@
     for copy in parts[0]:
         copy.start()
 
-    far.near()
     for part in range(2):
         for copy in parts[1 + part]:
             copy.wait_recv()
@@ -430,11 +435,9 @@
         sum_b[pair] = total.astype(BF16)
         start_towards(lates, part)
 
-    visit_images(1, far)
-    visit_images(2, far)
-    far.far()
-    visit_images(3, far)
-    image_out[...] = unit_back(image_ref[...].astype(F32), image_sum[...])
+    image_back.wait_recv()
+    incoming = image_sum[...] + image_back_in[...].astype(F32)
+    image_out[...] = unit_back(image_ref[...].astype(F32), incoming)
 
     for copy in parts[0]:
         copy.wait_recv()
@@ -451,11 +454,11 @@
         total = total + far_b[n].astype(F32)
     head_out[:, 128:256] = total[0:D_DEV]
 
-    for gather in (img, txt, far, *grds):
+    for gather in (img, txt, *grds):
         gather.finish()
     for copy in pieces + halves + lates + parts[0] + parts[1] + parts[2]:
         copy.wait_send()
-    for copy in (text_across, text_back):
+    for copy in (text_across, text_back, image_across, image_back):
         copy.wait_send()
 
 
@@ -482,11 +485,14 @@
             pltpu.VMEM((8, ROWS, D), BF16),
             pltpu.VMEM((8, ROWS, D), BF16),
             pltpu.VMEM((8, ROWS, D), BF16),
-            pltpu.VMEM((8, ROWS, D), BF16),
+            pltpu.VMEM((ROWS, D), BF16),
+            pltpu.VMEM((ROWS, D), BF16),
             pltpu.VMEM((ROWS, D), F32),
             pltpu.VMEM((ROWS, D), F32),
             pltpu.VMEM((ROWS, D), F32),
             pltpu.VMEM((ROWS, D), F32),
+            pltpu.VMEM((ROWS, D), BF16),
+            pltpu.VMEM((ROWS, D), BF16),
             pltpu.VMEM((ROWS, D), BF16),
             pltpu.VMEM((ROWS, D), BF16),
             pltpu.VMEM((8, 2 * FF_PAD, ROWS), BF16),
@@ -511,10 +517,8 @@
             dma((sends,)),
             dma((sends,)),
             dma((sends,)),
-            dma((sends,)),
-            dma((sends,)),
-            dma((2,)),
-            dma((2,)),
+            dma((4,)),
+            dma((4,)),
             dma((7,)),
             dma((7,)),
             dma((6,)),

time: 79 us -> 82.3 us (1.042)
  the two profiles are of different devices: /device:TPU:1 before, /device:TPU:34 now
where the time goes in v6:
time: 82.3 us; the launch traced here: 82.1 us
  Pallas kernels  80.2 us (97%)
  between operations  1.93 us (2%)
    pallas_call x1, Pallas kernels, local(): pl.pallas_call(kernel, out_shape=(jax.ShapeDtypeStruct((ROWS, D), F32), j...  78.2 us
    pallas_call x1, Pallas kernels, local(): pl.pallas_call(settle, out_shape=(jax.ShapeDtypeStruct((ROWS, D), F32), j...  1.95 us

profile of v6, /device:TPU:34, one launch (start us, length us, event | category | flops | bytes accessed | tf_op | source)
XLA Modules:
  0.0 82.1 jit_solution(16631460472016090365)
XLA Ops:
  1.9 78.2 %shard_map.77 = (f32[128,1152]{1,0:T(8,128)}, f32[72,269]{1,0:T(8,128)}) custom-call(bf16[128,1152]{1,0:T(8,128)(2,1)} %image_ref.1, bf16[4304,128]{1,0:T(8,128)(2,1)} %bitcast.2, bf16[4304,1152]{1,0:T(8,128)(2,1)} %weight_ref.1, s32[1,128]{1,0:T(1,128)} %positive_ref.1, f32[1]{0:T(128)S(6)} %copy.8.scale_ref, f32[1]{0:T(128)S(6)} %copy.9.bias_ref), custom_call_target="tpu_custom_call" | custom-call | tf_op jit(solution)/shard_map/pallas_call | solution.py:475
  80.2 2.0 %shard_map.78 = (f32[128,1152]{1,0:T(8,128)}, f32[72,269]{1,0:T(8,128)}) custom-call(f32[128,1152]{1,0:T(8,128)} %get-tuple-element.6.image_ref, f32[72,269]{1,0:T(8,128)} %get-tuple-element.7.head_ref), custom_call_target="tpu_custom_call" | custom-call | tf_op jit(solution)/shard_map/pallas_call | solution.py:540

commit v7 on v5

--- a/solution.py
+++ b/solution.py
@@ -280,7 +280,6 @@
         img.got(*ORDER[n][1])
         visit_texts(n)
     img.far()
-    txt.send(0, 1, 2, 3)
     text_across.wait_recv()
     far.send(6)
     for n in range(3):
@@ -289,6 +288,7 @@
     visit_far_texts(3)
     text_back_out[...] = far_sum[...].astype(BF16)
     text_back.start()
+    txt.send(0, 1, 2, 3)
     visit_texts(3)
     visit_images(0, txt)
     visit_images(0, far)
@@ -392,11 +392,21 @@
     grds[1].got(*ORDER[3][1])
     send_sums(1)
 
+    def settle_late(part):
+        for copy in parts[1 + part]:
+            copy.wait_recv()
+        pair = slice(2 * part, 2 * part + 2)
+        total = part_b[z, pair].astype(F32)
+        for n in range(7):
+            total = total + in_b[n, pair].astype(F32)
+        sum_b[pair] = total.astype(BF16)
+        start_towards(lates, part)
+
     visit_images(1, txt)
     visit_images(2, txt)
+    settle_late(0)
     txt.far()
     far.pass_on()
-    visit_images(3, txt)
 
     for copy in halves:
         copy.wait_recv()
@@ -419,17 +429,9 @@
     for copy in parts[0]:
         copy.start()
 
+    settle_late(1)
     far.near()
-    for part in range(2):
-        for copy in parts[1 + part]:
-            copy.wait_recv()
-        pair = slice(2 * part, 2 * part + 2)
-        total = part_b[z, pair].astype(F32)
-        for n in range(7):
-            total = total + in_b[n, pair].astype(F32)
-        sum_b[pair] = total.astype(BF16)
-        start_towards(lates, part)
-
+    visit_images(3, txt)
     visit_images(1, far)
     visit_images(2, far)
     far.far()

time: 79 us -> 77.5 us (0.981)
  Pallas kernels: 76.9 us -> 75.2 us
    pallas_call x1, Pallas kernels: 74.9 us -> 73.2 us  [local(): pl.pallas_call(kernel, out_shape=(jax.ShapeDtypeStruct((ROWS, D), F32), j...]
where the time goes in v7:
time: 77.5 us; the launch traced here: 77.1 us
  Pallas kernels  75.2 us (97%)
  between operations  1.93 us (2%)
    pallas_call x1, Pallas kernels, local(): pl.pallas_call(kernel, out_shape=(jax.ShapeDtypeStruct((ROWS, D), F32), j...  73.2 us
    pallas_call x1, Pallas kernels, local(): pl.pallas_call(settle, out_shape=(jax.ShapeDtypeStruct((ROWS, D), F32), j...  1.95 us

profile of v7, /device:TPU:1, one launch (start us, length us, event | category | flops | bytes accessed | tf_op | source)
XLA Modules:
  0.0 77.1 jit_solution(9703297193163749261)
XLA Ops:
  1.9 73.2 %shard_map.77 = (f32[128,1152]{1,0:T(8,128)}, f32[72,269]{1,0:T(8,128)}) custom-call(bf16[128,1152]{1,0:T(8,128)(2,1)} %image_ref.1, bf16[4304,128]{1,0:T(8,128)(2,1)} %bitcast.2, bf16[4304,1152]{1,0:T(8,128)(2,1)} %weight_ref.1, s32[1,128]{1,0:T(1,128)} %positive_ref.1, f32[1]{0:T(128)S(6)} %copy.8.scale_ref, f32[1]{0:T(128)S(6)} %copy.9.bias_ref), custom_call_target="tpu_custom_call" | custom-call | tf_op jit(solution)/shard_map/pallas_call | solution.py:474
  75.2 2.0 %shard_map.78 = (f32[128,1152]{1,0:T(8,128)}, f32[72,269]{1,0:T(8,128)}) custom-call(f32[128,1152]{1,0:T(8,128)} %get-tuple-element.6.image_ref, f32[72,269]{1,0:T(8,128)} %get-tuple-element.7.head_ref), custom_call_target="tpu_custom_call" | custom-call | tf_op jit(solution)/shard_map/pallas_call | solution.py:538

commit v8 on v7

--- a/solution.py
+++ b/solution.py
@@ -276,10 +276,10 @@
         block = chip(gather.buf, ORDER[n][0])
         visit(images[own], block, image_sum, own_label is not None, own_label)
 
+    img.far()
     for n in range(3):
         img.got(*ORDER[n][1])
         visit_texts(n)
-    img.far()
     text_across.wait_recv()
     far.send(6)
     for n in range(3):
@@ -317,8 +317,8 @@
     grds[0].near()
     add_head(0, 1)
     add_head(0, 2)
+    grds[1].pass_on()
     grds[0].far()
-    grds[1].pass_on()
 
     FLIPS = [(0, 1), (1, 0), (1, 1)]
     ROUND = (1, 7, 2, 6, 3, 5, 4)

time: 77.5 us -> 77.9 us (level)
  no operation moved by 1% of the time
where the time goes in v8:
time: 77.9 us; the launch traced here: 77.8 us
  Pallas kernels  75.8 us (97%)
  between operations  1.93 us (2%)
    pallas_call x1, Pallas kernels, local(): pl.pallas_call(kernel, out_shape=(jax.ShapeDtypeStruct((ROWS, D), F32), j...  73.9 us
    pallas_call x1, Pallas kernels, local(): pl.pallas_call(settle, out_shape=(jax.ShapeDtypeStruct((ROWS, D), F32), j...  1.95 us

profile of v8, /device:TPU:1, one launch (start us, length us, event | category | flops | bytes accessed | tf_op | source)
XLA Modules:
  0.0 77.8 jit_solution(8552759266647947573)
XLA Ops:
  1.9 73.9 %shard_map.77 = (f32[128,1152]{1,0:T(8,128)}, f32[72,269]{1,0:T(8,128)}) custom-call(bf16[128,1152]{1,0:T(8,128)(2,1)} %image_ref.1, bf16[4304,128]{1,0:T(8,128)(2,1)} %bitcast.2, bf16[4304,1152]{1,0:T(8,128)(2,1)} %weight_ref.1, s32[1,128]{1,0:T(1,128)} %positive_ref.1, f32[1]{0:T(128)S(6)} %copy.8.scale_ref, f32[1]{0:T(128)S(6)} %copy.9.bias_ref), custom_call_target="tpu_custom_call" | custom-call | tf_op jit(solution)/shard_map/pallas_call | solution.py:474
  75.8 2.0 %shard_map.78 = (f32[128,1152]{1,0:T(8,128)}, f32[72,269]{1,0:T(8,128)}) custom-call(f32[128,1152]{1,0:T(8,128)} %get-tuple-element.6.image_ref, f32[72,269]{1,0:T(8,128)} %get-tuple-element.7.head_ref), custom_call_target="tpu_custom_call" | custom-call | tf_op jit(solution)/shard_map/pallas_call | solution.py:538
